TPU v7x, 32 devices: a whole 2x2x4 slice. The times are simulated.
32 devices in a mesh: rep: 16 (over z, y, x), shard: 2 (over core).
Axes of the slice: x: 2, y: 2, z: 4, core: 2. Of those that a mesh axis runs over, the one named last changes fastest.
Arguments:
- images: bfloat16 [192, 196, 512], P(('rep', 'shard')), may hold values from -6 to 6
- cotangent: bfloat16 [192, 196, 512], P(('rep', 'shard')), may hold values from -6 to 6
- window_map: int32 [2, 196], replicated, may hold values from 0 to 195, as said below
- shift_mask: int32 [4, 49, 49], replicated, may hold values from 0 to 1, as said below
- rel_index: int32 [49, 49], replicated, may hold values from 0 to 168, as said below
- attend_weight: float32 [2, 512, 1536], P(None, 'shard'), may hold values from -0.25 to 0.25
- attend_moment: float32 [2, 512, 1536], P(None, 'shard'), may hold values from -128 to 128
- attend_square: float32 [2, 512, 1536], P(None, 'shard'), may hold values from 37.632 to 150.528
- output_weight: float32 [2, 512, 512], P(None, 'shard'), may hold values from -0.75 to 0.75
- output_moment: float32 [2, 512, 512], P(None, 'shard'), may hold values from -40 to 40
- output_square: float32 [2, 512, 512], P(None, 'shard'), may hold values from 3.38688 to 13.54752
- expand_weight: float32 [2, 512, 2048], P(None, 'shard'), may hold values from -0.25 to 0.25
- expand_moment: float32 [2, 512, 2048], P(None, 'shard'), may hold values from -40 to 40
- expand_square: float32 [2, 512, 2048], P(None, 'shard'), may hold values from 3.38688 to 13.54752
- reduce_weight: float32 [2, 2048, 512], P(None, 'shard'), may hold values from -0.125 to 0.125
- reduce_moment: float32 [2, 2048, 512], P(None, 'shard'), may hold values from -80 to 80
- reduce_square: float32 [2, 2048, 512], P(None, 'shard'), may hold values from 13.54752 to 54.19008
- bias_table: float32 [2, 16, 169], P(None, 'shard'), may hold values from -6 to 6
- table_moment: float32 [2, 16, 169], P(None, 'shard'), may hold values from -112 to 112
- table_square: float32 [2, 16, 169], P(None, 'shard'), may hold values from 27.09504 to 109.1328
- layer_vectors: float32 [2, 6, 512], P(None, None, 'shard')
- vector_moment: float32 [2, 6, 512], P(None, None, 'shard'), may hold values from -128 to 128
- vector_square: float32 [2, 6, 512], P(None, None, 'shard'), may hold values from 37.632 to 150.528
- wide_bias: float32 [2, 3072], P(None, 'shard'), may hold values from -3 to 3
- biases_moment: float32 [2, 3072], P(None, 'shard'), may hold values from -80 to 80
- biases_square: float32 [2, 3072], P(None, 'shard'), may hold values from 13.54752 to 54.19008
Outputs:
- block_out: bfloat16 [192, 196, 512], P(('rep', 'shard'))
- input_grad: float32 [192, 196, 512], P(('rep', 'shard'))
- moment_attend: float32 [2, 512, 1536], P(None, 'shard')
- square_attend: float32 [2, 512, 1536], P(None, 'shard')
- updated_attend: float32 [2, 512, 1536], P(None, 'shard')
- moment_output: float32 [2, 512, 512], P(None, 'shard')
- square_output: float32 [2, 512, 512], P(None, 'shard')
- updated_output: float32 [2, 512, 512], P(None, 'shard')
- moment_expand: float32 [2, 512, 2048], P(None, 'shard')
- square_expand: float32 [2, 512, 2048], P(None, 'shard')
- updated_expand: float32 [2, 512, 2048], P(None, 'shard')
- moment_reduce: float32 [2, 2048, 512], P(None, 'shard')
- square_reduce: float32 [2, 2048, 512], P(None, 'shard')
- updated_reduce: float32 [2, 2048, 512], P(None, 'shard')
- moment_table: float32 [2, 16, 169], P(None, 'shard')
- square_table: float32 [2, 16, 169], P(None, 'shard')
- updated_table: float32 [2, 16, 169], P(None, 'shard')
- moment_vectors: float32 [2, 6, 512], P(None, None, 'shard')
- square_vectors: float32 [2, 6, 512], P(None, None, 'shard')
- updated_vectors: float32 [2, 6, 512], P(None, None, 'shard')
- moment_biases: float32 [2, 3072], P(None, 'shard')
- square_biases: float32 [2, 3072], P(None, 'shard')
- updated_biases: float32 [2, 3072], P(None, 'shard')
Inputs may be any that keep to these rules, and one draw needn't show every extreme that they name: `window_map`: each row is a permutation of the 196 tokens, slots listed window by window; within a window slot j sits at the same grid place in every window, and odd rows are even rows cyclically shifted on the 14 x 14 grid. `shift_mask`: 1 where two slots of a window lie in different regions of the shifted grid. `rel_index`: pairs of slots with equal grid offset share a row, different offsets take different rows.
All inputs are finite; a program needn't handle non-finite values.
Results may differ from a plain program's by a relative error of at most 0.028.
Values may be sent and summed in bfloat16 or wider, within the bound.
A program may use at most 320 MiB of HBM per device.

v0:
```python
import jax
import jax.numpy as jnp
from jax import lax
from jax.sharding import PartitionSpec as P

D = 512
FF = 2048
STEP = 10


def norm_rows(v, gain, shift):
    mean = jnp.mean(v, axis=-1, keepdims=True)
    centered = v - mean
    var = jnp.mean(centered * centered, axis=-1, keepdims=True)
    return centered * lax.rsqrt(var + 1e-05) * gain + shift


def gelu_exact(v):
    return 0.5 * v * (1.0 + jax.scipy.special.erf(v * 0.7071067811865476))


def matmul(left, right):
    return jnp.einsum("bti,in->btn", left, right, preferred_element_type=jnp.float32)


def matmul_back(left, right):
    return jnp.einsum("btn,in->bti", left, right, preferred_element_type=jnp.float32)


def weight_grad(left, right):
    return jnp.einsum("bti,btn->in", left, right, preferred_element_type=jnp.float32)


def fetch_forward(masters, layer):
    attend, output, expand, shrink, table, vectors, biases = (
        item[layer].astype(jnp.bfloat16) for item in masters
    )
    return (
        lax.all_gather(attend, "shard", axis=0, tiled=True),
        lax.all_gather(output, "shard", axis=0, tiled=True),
        lax.all_gather(expand, "shard", axis=0, tiled=True),
        lax.all_gather(shrink, "shard", axis=0, tiled=True),
        lax.all_gather(table, "shard", axis=0, tiled=True),
        lax.all_gather(vectors, "shard", axis=1, tiled=True),
        lax.all_gather(biases, "shard", axis=0, tiled=True),
    )


def fetch_backward(masters, layer):
    attend, output, expand, shrink, table, vectors, biases = (
        item[layer].astype(jnp.bfloat16) for item in masters
    )
    return (
        lax.all_gather(attend, "shard", axis=0, tiled=True),
        lax.all_gather(output, "shard", axis=0, tiled=True),
        lax.all_gather(expand, "shard", axis=0, tiled=True),
        lax.all_gather(shrink, "shard", axis=0, tiled=True),
        lax.all_gather(table, "shard", axis=0, tiled=True),
        lax.all_gather(vectors, "shard", axis=1, tiled=True),
        lax.all_gather(biases, "shard", axis=0, tiled=True),
    )


def relative_table(rel_index, rows):
    return (rel_index[:, :, None] == jnp.arange(rows, dtype=jnp.int32)[None, None, :]).astype(
        jnp.float32
    )


def split_heads(lifted, windows, heads):
    count, tokens, triple = lifted.shape
    depth = triple // (3 * heads)
    parts = lifted.reshape(count, windows, tokens // windows, 3, heads, depth)
    return (parts[:, :, :, 0], parts[:, :, :, 1], parts[:, :, :, 2], depth)


def window_scores(query, keys, table, onehot, penalty, depth):
    position = jnp.einsum(
        "hr,ijr->hij", table.astype(jnp.float32), onehot, precision=lax.Precision.HIGHEST
    )
    scores = jnp.einsum(
        "bwihc,bwjhc->bwhij", query, keys, preferred_element_type=jnp.float32
    ) * depth ** (-0.5)
    return scores + position[None, None] + penalty[None, :, None]


def forward_layer(state, order, penalty, rel_index, weights):
    attend, output, expand, shrink, table, vectors, biases = weights
    gains = vectors.astype(jnp.float32)
    offsets = biases.astype(jnp.float32)
    width = attend.shape[0]
    count, tokens, _ = state.shape
    windows = penalty.shape[0]
    heads = table.shape[0]
    onehot = relative_table(rel_index, table.shape[1])
    slots_in = jnp.take(state, order, axis=1)
    normed = norm_rows(slots_in, gains[0], gains[1]).astype(jnp.bfloat16)
    qkv_bias = jnp.concatenate(
        [offsets[:width], jnp.zeros((width,), jnp.float32), offsets[width : 2 * width]]
    )
    lifted = (matmul(normed, attend) + qkv_bias).astype(jnp.bfloat16)
    query, keys, values, depth = split_heads(lifted, windows, heads)
    scores = window_scores(query, keys, table, onehot, penalty, depth)
    top = jnp.max(scores, axis=-1, keepdims=True)
    logsum = top + jnp.log(jnp.sum(jnp.exp(scores - top), axis=-1, keepdims=True))
    probs = jnp.exp(scores - logsum).astype(jnp.bfloat16)
    mixed = jnp.einsum("bwhij,bwjhc->bwihc", probs, values, preferred_element_type=jnp.float32)
    mixed = mixed.reshape(count, tokens, width).astype(jnp.bfloat16)
    middle = slots_in + matmul(mixed, output) + gains[2]
    normed_two = norm_rows(middle, gains[3], gains[4]).astype(jnp.bfloat16)
    hidden = matmul(normed_two, expand) + offsets[2 * width :]
    activated = gelu_exact(hidden).astype(jnp.bfloat16)
    slots_out = middle + matmul(activated, shrink) + gains[5]
    new_state = jnp.take(slots_out, jnp.argsort(order), axis=1)
    return (
        new_state,
        (slots_in, normed, lifted, logsum, mixed, middle, normed_two, hidden, activated),
    )


def backward_layer(grad_state, order, penalty, rel_index, weights, saved):
    attend, output, expand, shrink, table, vectors, biases = weights
    gains = vectors.astype(jnp.float32)
    slots_in, normed, lifted, logsum, mixed, middle, normed_two, hidden, activated = saved
    width = attend.shape[0]
    count, tokens, _ = grad_state.shape
    windows = penalty.shape[0]
    heads = table.shape[0]
    onehot = relative_table(rel_index, table.shape[1])
    grad_slots = jnp.take(grad_state, order, axis=1)
    grad_top = grad_slots.astype(jnp.bfloat16)
    grad_last = jnp.sum(grad_top, axis=(0, 1), dtype=jnp.float32)
    grad_shrink = weight_grad(activated, grad_top)
    grad_act = matmul_back(grad_top, shrink)
    _, gelu_pull = jax.vjp(gelu_exact, hidden)
    grad_hidden = gelu_pull(grad_act)[0].astype(jnp.bfloat16)
    grad_fbias = jnp.sum(grad_hidden, axis=(0, 1), dtype=jnp.float32)
    grad_expand = weight_grad(normed_two, grad_hidden)
    grad_normed_two = matmul_back(grad_hidden, expand)
    _, norm_pull_two = jax.vjp(norm_rows, middle, gains[3], gains[4])
    grad_middle, grad_gain_two, grad_shift_two = norm_pull_two(grad_normed_two)
    grad_middle = grad_middle + grad_slots
    grad_branch = grad_middle.astype(jnp.bfloat16)
    grad_pbias = jnp.sum(grad_branch, axis=(0, 1), dtype=jnp.float32)
    grad_output = weight_grad(mixed, grad_branch)
    grad_mixed = matmul_back(grad_branch, output).astype(jnp.bfloat16)
    query, keys, values, depth = split_heads(lifted, windows, heads)
    grad_heads = grad_mixed.reshape(query.shape)
    scores = window_scores(query, keys, table, onehot, penalty, depth)
    probs_full = jnp.exp(scores - logsum)
    probs = probs_full.astype(jnp.bfloat16)
    grad_values = jnp.einsum(
        "bwhij,bwihc->bwjhc", probs, grad_heads, preferred_element_type=jnp.float32
    )
    grad_probs = jnp.einsum(
        "bwihc,bwjhc->bwhij", grad_heads, values, preferred_element_type=jnp.float32
    )
    inner = jnp.sum(probs_full * grad_probs, axis=-1, keepdims=True)
    grad_scores = (probs_full * (grad_probs - inner)).astype(jnp.bfloat16)
    pair_sums = jnp.sum(grad_scores, axis=(0, 1), dtype=jnp.float32)
    grad_table = jnp.einsum("hij,ijr->hr", pair_sums, onehot, precision=lax.Precision.HIGHEST)
    grad_query = jnp.einsum(
        "bwhij,bwjhc->bwihc", grad_scores, keys, preferred_element_type=jnp.float32
    ) * depth ** (-0.5)
    grad_keys = jnp.einsum(
        "bwhij,bwihc->bwjhc", grad_scores, query, preferred_element_type=jnp.float32
    ) * depth ** (-0.5)
    grad_lifted = jnp.stack([grad_query, grad_keys, grad_values], axis=3)
    grad_lifted = grad_lifted.reshape(count, tokens, 3 * width).astype(jnp.bfloat16)
    grad_qbias = jnp.sum(grad_lifted[:, :, :width], axis=(0, 1), dtype=jnp.float32)
    grad_vbias = jnp.sum(grad_lifted[:, :, 2 * width :], axis=(0, 1), dtype=jnp.float32)
    grad_attend = weight_grad(normed, grad_lifted)
    grad_normed = matmul_back(grad_lifted, attend)
    _, norm_pull_one = jax.vjp(norm_rows, slots_in, gains[0], gains[1])
    grad_in, grad_gain_one, grad_shift_one = norm_pull_one(grad_normed)
    grad_in = grad_in + grad_middle
    grad_before = jnp.take(grad_in, jnp.argsort(order), axis=1)
    grad_vectors = jnp.stack(
        [grad_gain_one, grad_shift_one, grad_pbias, grad_gain_two, grad_shift_two, grad_last]
    )
    grad_biases = jnp.concatenate([grad_qbias, grad_vbias, grad_fbias])
    return (
        grad_before,
        (grad_attend, grad_output, grad_expand, grad_shrink, grad_table, grad_vectors, grad_biases),
    )


def adam(weight, moment, square, grad, rate, decay):
    moment_new = 0.9 * moment + 0.1 * grad
    square_new = 0.999 * square + 0.001 * grad * grad
    first_hat = moment_new / (1.0 - 0.9**STEP)
    second_hat = square_new / (1.0 - 0.999**STEP)
    weight_new = weight - rate * (first_hat / (jnp.sqrt(second_hat) + 1e-08) + decay * weight)
    return (moment_new, square_new, weight_new)


def shards(
    images,
    cotangent,
    window_map,
    shift_mask,
    rel_index,
    attend_weight,
    attend_moment,
    attend_square,
    output_weight,
    output_moment,
    output_square,
    expand_weight,
    expand_moment,
    expand_square,
    reduce_weight,
    reduce_moment,
    reduce_square,
    bias_table,
    table_moment,
    table_square,
    layer_vectors,
    vector_moment,
    vector_square,
    wide_bias,
    biases_moment,
    biases_square,
):
    masters = (
        attend_weight,
        output_weight,
        expand_weight,
        reduce_weight,
        bias_table,
        layer_vectors,
        wide_bias,
    )
    layers = attend_weight.shape[0]
    mask_term = -100.0 * shift_mask.astype(jnp.float32)
    state = images.astype(jnp.float32)
    saved_all = []
    held_weights = []
    for layer in range(layers):
        weights = fetch_forward(masters, layer)
        state, saved = forward_layer(
            state, window_map[layer], mask_term * float(layer % 2), rel_index, weights
        )
        saved_all.append(saved)
        held_weights.append(None)
    block_out = state.astype(jnp.bfloat16)
    grad_state = cotangent.astype(jnp.float32)
    shares = [None] * layers
    for layer in reversed(range(layers)):
        weights = fetch_backward(masters, layer)
        grad_state, grads = backward_layer(
            grad_state,
            window_map[layer],
            mask_term * float(layer % 2),
            rel_index,
            weights,
            saved_all[layer],
        )
        g_attend, g_output, g_expand, g_shrink, g_table, g_vectors, g_biases = grads
        owned = (
            lax.psum_scatter(
                g_attend.astype(jnp.bfloat16), "shard", scatter_dimension=0, tiled=True
            ).astype(jnp.float32),
            lax.psum_scatter(
                g_output.astype(jnp.bfloat16), "shard", scatter_dimension=0, tiled=True
            ).astype(jnp.float32),
            lax.psum_scatter(
                g_expand.astype(jnp.bfloat16), "shard", scatter_dimension=0, tiled=True
            ).astype(jnp.float32),
            lax.psum_scatter(
                g_shrink.astype(jnp.bfloat16), "shard", scatter_dimension=0, tiled=True
            ).astype(jnp.float32),
            lax.psum_scatter(
                g_table.astype(jnp.bfloat16), "shard", scatter_dimension=0, tiled=True
            ).astype(jnp.float32),
            lax.psum_scatter(
                g_vectors.astype(jnp.bfloat16), "shard", scatter_dimension=1, tiled=True
            ).astype(jnp.float32),
            lax.psum_scatter(
                g_biases.astype(jnp.bfloat16), "shard", scatter_dimension=0, tiled=True
            ).astype(jnp.float32),
        )
        o_attend, o_output, o_expand, o_shrink, o_table, o_vectors, o_biases = owned
        owned = (
            lax.psum(o_attend.astype(jnp.bfloat16), "rep").astype(jnp.float32),
            lax.psum(o_output.astype(jnp.bfloat16), "rep").astype(jnp.float32),
            lax.psum(o_expand.astype(jnp.bfloat16), "rep").astype(jnp.float32),
            lax.psum(o_shrink.astype(jnp.bfloat16), "rep").astype(jnp.float32),
            lax.psum(o_table.astype(jnp.bfloat16), "rep").astype(jnp.float32),
            lax.psum(o_vectors.astype(jnp.bfloat16), "rep").astype(jnp.float32),
            lax.psum(o_biases.astype(jnp.bfloat16), "rep").astype(jnp.float32),
        )
        shares[layer] = owned
    stacked = tuple(
        (jnp.stack([shares[layer][index] for layer in range(layers)]) for index in range(7))
    )
    ma, sa, wa = adam(
        attend_weight, attend_moment, attend_square, stacked[0], 3.0 * D ** (-0.5), 0.05
    )
    mo, so, wo = adam(
        output_weight, output_moment, output_square, stacked[1], 3.0 * (8.0 / D) ** 0.5, 0.05
    )
    me, se, we = adam(
        expand_weight, expand_moment, expand_square, stacked[2], 3.0 * D ** (-0.5), 0.05
    )
    mr, sr, wr = adam(
        reduce_weight, reduce_moment, reduce_square, stacked[3], 3.0 * FF ** (-0.5), 0.05
    )
    mt, st, wt = adam(bias_table, table_moment, table_square, stacked[4], 3.0, 0.0)
    mv, sv, wv = adam(layer_vectors, vector_moment, vector_square, stacked[5], 1.0, 0.0)
    mb, sb, wb = adam(wide_bias, biases_moment, biases_square, stacked[6], 1.5, 0.0)
    return (
        block_out,
        grad_state,
        ma,
        sa,
        wa,
        mo,
        so,
        wo,
        me,
        se,
        we,
        mr,
        sr,
        wr,
        mt,
        st,
        wt,
        mv,
        sv,
        wv,
        mb,
        sb,
        wb,
    )


def solution(mesh):
    return jax.shard_map(
        shards,
        mesh=mesh,
        in_specs=(
            P(("rep", "shard"), None, None),
            P(("rep", "shard"), None, None),
            P(),
            P(),
            P(),
            P(None, "shard", None),
            P(None, "shard", None),
            P(None, "shard", None),
            P(None, "shard", None),
            P(None, "shard", None),
            P(None, "shard", None),
            P(None, "shard", None),
            P(None, "shard", None),
            P(None, "shard", None),
            P(None, "shard", None),
            P(None, "shard", None),
            P(None, "shard", None),
            P(None, "shard", None),
            P(None, "shard", None),
            P(None, "shard", None),
            P(None, None, "shard"),
            P(None, None, "shard"),
            P(None, None, "shard"),
            P(None, "shard"),
            P(None, "shard"),
            P(None, "shard"),
        ),
        out_specs=(
            P(("rep", "shard"), None, None),
            P(("rep", "shard"), None, None),
            P(None, "shard", None),
            P(None, "shard", None),
            P(None, "shard", None),
            P(None, "shard", None),
            P(None, "shard", None),
            P(None, "shard", None),
            P(None, "shard", None),
            P(None, "shard", None),
            P(None, "shard", None),
            P(None, "shard", None),
            P(None, "shard", None),
            P(None, "shard", None),
            P(None, "shard", None),
            P(None, "shard", None),
            P(None, "shard", None),
            P(None, None, "shard"),
            P(None, None, "shard"),
            P(None, None, "shard"),
            P(None, "shard"),
            P(None, "shard"),
            P(None, "shard"),
        ),
        check_vma=False,
    )
```

profile of v0, /device:TPU:0, one launch (start us, length us, event | category | flops | bytes accessed | tf_op | source)
XLA Modules:
  0.0 905.6 jit_solution(5281696477644745276)
XLA Ops:
  60.1 4.6 gather_fusion.4
  64.7 5.0 fusion.132
  69.8 5.5 add_convert_fusion.3
  75.3 12.0 %reshape.418 = bf16[6,4,49,3,16,32]{5,4,3,2,1,0:T(8,128)(2,1)} reshape(bf16[6,196,1536]{2,1,0:T(8,128)(2,1)} %add_convert_fusion.3) | data formatting | bytes 7225344 | tf_op jit(solution)/shard_map/reshape | solution.py:73
  87.3 12.0 %fusion.142 = (bf16[6,4,49,1,16,32]{5,4,3,2,1,0:T(8,128)(2,1)}, bf16[6,4,49,1,16,32]{5,4,3,2,1,0:T(8,128)(2,1)}, bf16[6,4,49,1,16,32]{5,4,3,2,1,0:T(8,128)(2,1)}) fusion(bf16[6,4,49,3,16,32]{5,4,3,2,1,0:T(8,128)(2,1)} %reshape.418), kind=kLoop, calls=%fused_computation.272 | loop fusion | bytes 7225344 | tf_op jit(solution)/shard_map/slice | solution.py:74
  99.3 7.4 copy.271
  106.7 7.4 copy.270
  114.0 7.4 copy.272
  121.5 6.1 fusion.155
  134.5 5.7 copy.196
  140.2 5.5 convert_element_type.315
  150.2 9.2 %multiply_convert_fusion.3 = (bf16[6,196,2048]{2,1,0:T(8,128)(2,1)}, f32[6,196,2048]{2,1,0:T(8,128)}) fusion(f32[2048]{0:T(1024)S(1)} %bitcast.369, bf16[1,512,2048]{2,1,0:T(8,128)(2,1)} %all-gather.23.cloned.1.call-done, f32[6,196,512]{2,1,0:T(8,128)} %copy-done.6, f32[512]{0:T(512)S(1)} %bitcast.382, f32[512]{0:T(512)S(1)} %bitcast.341, ...), kind=kOutput, calls=%fused_computation.24 | convolution fusion | flops 2483712000 | bytes 18977984 | tf_op jit(solution)/shard_map/bti,in->btn/dot_general | solution.py:23
  159.5 5.7 add_add_fusion.9
  178.3 5.5 add_convert_fusion.2
  183.8 11.9 %reshape.419 = bf16[6,4,49,3,16,32]{5,4,3,2,1,0:T(8,128)(2,1)} reshape(bf16[6,196,1536]{2,1,0:T(8,128)(2,1)} %add_convert_fusion.2) | data formatting | bytes 7225344 | tf_op jit(solution)/shard_map/reshape | solution.py:73
  195.7 11.4 %fusion.141 = (bf16[6,4,49,1,16,32]{5,4,3,2,1,0:T(8,128)(2,1)}, bf16[6,4,49,1,16,32]{5,4,3,2,1,0:T(8,128)(2,1)}, bf16[6,4,49,1,16,32]{5,4,3,2,1,0:T(8,128)(2,1)}) fusion(bf16[6,4,49,3,16,32]{5,4,3,2,1,0:T(8,128)(2,1)} %reshape.419), kind=kLoop, calls=%fused_computation.271 | loop fusion | bytes 7225344 | tf_op jit(solution)/shard_map/slice | solution.py:74
  207.1 7.4 copy.274
  214.5 7.4 copy.273
  221.8 7.6 copy.275
  229.4 6.1 fusion.157
  242.5 5.7 copy.207
  248.2 5.5 convert_element_type.332
  258.2 9.1 %multiply_convert_fusion.2 = (bf16[6,196,2048]{2,1,0:T(8,128)(2,1)}, f32[6,196,2048]{2,1,0:T(8,128)}) fusion(f32[2048]{0:T(1024)S(1)} %bitcast.371, bf16[1,512,2048]{2,1,0:T(8,128)(2,1)} %all-gather.29.cloned.1.call-done, f32[6,196,512]{2,1,0:T(8,128)} %copy-done.4, f32[512]{0:T(512)S(1)} %bitcast.384, f32[512]{0:T(512)S(1)} %bitcast.346, ...), kind=kOutput, calls=%fused_computation.22 | convolution fusion | flops 2483712000 | bytes 18977984 | tf_op jit(solution)/shard_map/bti,in->btn/dot_general | solution.py:23
  267.2 10.4 %fusion.159 = (bf16[2048]{0:T(1024)(128)(2,1)}, bf16[6,196,2048]{2,1,0:T(8,128)(2,1)S(1)}) fusion(bf16[6,196,512]{2,1,0:T(8,128)(2,1)} %get-tuple-element.147, bf16[1,2048,512]{2,1,0:T(8,128)(2,1)} %all-gather.31.cloned.1.call-done, f32[6,196,2048]{2,1,0:T(8,128)} %get-tuple-element.223, f32[2048]{0:T(1024)S(1)} %bitcast.372), kind=kOutput, calls=%fused_computation.289 | convolution fusion | flops 2502375424 | bytes 17764352 | tf_op jit(solution)/shard_map/btn,in->bti/dot_general | solution.py:27
  292.8 5.3 reshape.420
  298.1 7.4 copy.213
  305.5 9.9 %convert_bitcast_fusion.1 = bf16[6,4,49,1,16,32]{2,5,4,1,0,3:T(8,128)(2,1)} fusion(bf16[6,4,49,16,32]{2,4,3,1,0:T(8,128)(2,1)} %copy.213, f32[6,4,16,49,49]{3,4,2,1,0:T(8,128)} %copy-done.1, f32[6,4,16,49]{3,2,1,0:T(8,128)S(1)} %log_add_fusion), kind=kOutput, calls=%fused_computation.90 | convolution fusion | flops 61453056 | bytes 6171648 | tf_op jit(solution)/shard_map/bwhij,bwihc->bwjhc/dot_general | solution.py:152
  315.4 9.0 multiply_reduce_fusion.1
  324.4 9.8 %convert_reduce_fusion = (f32[16,49,49]{1,2,0:T(8,128)}, bf16[6,4,16,49,49]{3,4,2,1,0:T(8,128)(2,1)S(1)}) fusion(f32[6,4,16,49,49]{3,4,2,1,0:T(8,128)} %get-tuple-element.226, f32[6,4,16,49]{3,2,1,0:T(8,128)S(1)} %get-tuple-element.225, f32[6,4,16,49,49]{3,4,2,1,0:T(8,128)} %copy-done.1, f32[6,4,16,49]{3,2,1,0:T(8,128)S(1)} %log_add_fusion), kind=kLoop, calls=%fused_computation.8 | loop fusion | flops 5493488 | bytes 9524032 | tf_op jit(solution)/shard_map/reduce_sum | solution.py:160
  334.2 4.2 fusion.9
  341.6 9.7 %pad_maximum_fusion = bf16[6,4,49,3,16,32]{2,5,4,1,0,3:T(8,128)(2,1)} fusion(bf16[6,4,49,1,16,32]{2,5,4,1,0,3:T(8,128)(2,1)} %convert_bitcast_fusion.1, bf16[6,4,49,1,16,32]{2,5,4,1,0,3:T(8,128)(2,1)} %fusion.9, bf16[6,4,49,1,16,32]{2,5,4,1,0,3:T(8,128)(2,1)} %fusion.8), kind=kLoop, calls=%fused_computation.26 | loop fusion | flops 3612672 | bytes 7225344 | tf_op jit(solution)/shard_map/stack | solution.py:168
  351.2 12.4 %copy.218 = bf16[6,4,49,3,16,32]{2,1,5,4,3,0:T(4,128)(2,1)} copy(bf16[6,4,49,3,16,32]{2,5,4,1,0,3:T(8,128)(2,1)} %pad_maximum_fusion) | data formatting | bytes 7225344 | tf_op jit(solution)/shard_map/stack | solution.py:168
  363.6 13.4 %convert_element_type.345 = bf16[6,196,1536]{1,2,0:T(8,128)(2,1)} reshape(bf16[6,4,49,3,16,32]{2,1,5,4,3,0:T(4,128)(2,1)} %copy.218) | data formatting | bytes 7225344 | tf_op jit(solution)/shard_map/convert_element_type | solution.py:169
  377.0 6.6 fusion.124
  389.4 4.5 gather_fusion.5
  393.9 4.0 select_bitcast_fusion.1
  397.9 4.5 gather_fusion.6
  402.4 4.1 fusion.131
  406.5 10.7 %fusion.160 = (bf16[2048]{0:T(1024)(128)(2,1)}, bf16[6,196,2048]{2,1,0:T(8,128)(2,1)S(1)}) fusion(bf16[6,196,512]{2,1,0:T(8,128)(2,1)S(1)} %get-tuple-element.143, bf16[1,2048,512]{2,1,0:T(8,128)(2,1)S(1)} %copy-done.118, f32[6,196,2048]{2,1,0:T(8,128)} %get-tuple-element.217, f32[2048]{0:T(1024)S(1)} %bitcast.370), kind=kOutput, calls=%fused_computation.290 | convolution fusion | flops 2502375424 | bytes 17764352 | tf_op jit(solution)/shard_map/btn,in->bti/dot_general | solution.py:27
  428.7 6.7 fusion.33
  438.1 4.1 reshape.421
  442.2 7.5 copy.223
  449.8 12.7 %multiply_reduce_fusion = (f32[6,4,16,49]{3,2,1,0:T(8,128)S(1)}, f32[6,4,16,49,49]{3,4,2,1,0:T(8,128)}) fusion(f32[6,4,16,49,49]{3,4,2,1,0:T(8,128)} %copy-done, f32[6,4,16,49]{3,2,1,0:T(8,128)S(1)} %copy-done.27, bf16[6,4,49,16,32]{2,4,3,1,0:T(8,128)(2,1)} %copy.223, bf16[6,4,49,1,16,32]{2,5,4,1,0,3:T(8,128)(2,1)S(1)} %copy-done.12), kind=kOutput, calls=%fused_computation.11 | convolution fusion | flops 61754112 | bytes 9934848 | tf_op jit(solution)/shard_map/bwihc,bwjhc->bwhij/dot_general | solution.py:155
  462.5 9.8 %convert_reduce_fusion.1 = (f32[16,49,49]{1,2,0:T(8,128)}, bf16[6,4,16,49,49]{3,4,2,1,0:T(8,128)(2,1)S(1)}) fusion(f32[6,4,16,49,49]{3,4,2,1,0:T(8,128)} %get-tuple-element.230, f32[6,4,16,49]{3,2,1,0:T(8,128)S(1)} %get-tuple-element.229, f32[6,4,16,49,49]{3,4,2,1,0:T(8,128)} %copy-done, f32[6,4,16,49]{3,2,1,0:T(8,128)S(1)} %copy-done.27), kind=kLoop, calls=%fused_computation.9 | loop fusion | flops 5493488 | bytes 9524032 | tf_op jit(solution)/shard_map/reduce_sum | solution.py:160
  472.3 6.9 fusion.11
  479.2 5.5 fusion.10
  484.8 6.6 convert_bitcast_fusion
  491.4 9.6 %pad_maximum_fusion.1 = bf16[6,4,49,3,16,32]{2,5,4,1,0,3:T(8,128)(2,1)} fusion(bf16[6,4,49,1,16,32]{2,5,4,1,0,3:T(8,128)(2,1)} %convert_bitcast_fusion, bf16[6,4,49,1,16,32]{2,5,4,1,0,3:T(8,128)(2,1)} %fusion.11, bf16[6,4,49,1,16,32]{2,5,4,1,0,3:T(8,128)(2,1)} %fusion.10), kind=kLoop, calls=%fused_computation.27 | loop fusion | flops 3612672 | bytes 7225344 | tf_op jit(solution)/shard_map/stack | solution.py:168
  501.0 12.2 %copy.228 = bf16[6,4,49,3,16,32]{2,1,5,4,3,0:T(4,128)(2,1)} copy(bf16[6,4,49,3,16,32]{2,5,4,1,0,3:T(8,128)(2,1)} %pad_maximum_fusion.1) | data formatting | bytes 7225344 | tf_op jit(solution)/shard_map/stack | solution.py:168
  513.2 13.7 %convert_element_type.351 = bf16[6,196,1536]{1,2,0:T(8,128)(2,1)} reshape(bf16[6,4,49,3,16,32]{2,1,5,4,3,0:T(4,128)(2,1)} %copy.228) | data formatting | bytes 7225344 | tf_op jit(solution)/shard_map/convert_element_type | solution.py:169
  527.0 6.7 fusion.32
  533.8 7.0 bitcast_convert_fusion
  540.9 8.1 bitcast_convert_fusion.2
  549.5 7.0 bitcast_convert_fusion.1
  556.7 8.0 bitcast_convert_fusion.3
  570.7 7.7 fusion.122
  586.7 13.6 %reduce-scatter.21.cloned.1.call-done = bf16[256,2048]{1,0:T(8,128)(2,1)} async-done(((bf16[512,2048]{1,0:T(8,128)(2,1)}), bf16[256,2048]{1,0:T(8,128)(2,1)}) %reduce-scatter.21.cloned.1.call-update) | async-done | bytes 1048592 | tf_op jit(solution)/shard_map/reduce_scatter | solution.py:267
  602.2 6.5 add_add_fusion.8
  637.9 7.1 reduce-scatter.33.cloned.1.call-done
  645.1 80.8 %all-reduce.2 = (bf16[1,8,169]{2,1,0:T(8,128)(2,1)S(1)}, bf16[1,8,169]{2,1,0:T(8,128)(2,1)S(1)}, bf16[1,6,256]{2,1,0:T(8,128)(2,1)S(1)}, bf16[1,6,256]{2,1,0:T(8...) all-reduce(bf16[1,8,169]{2,1,0:T(8,128)(2,1)} %bitcast.377, ...), channel_id=1, replica_groups=mesh['rep'=16,'shard'=2] {'rep'}, use_global_device_ids=true, to_apply=%region_45.47 | all-reduce | flops 8848 | bytes 35392 | tf_op jit(solution)/shard_map/psum | solution.py:289
  729.0 140.5 %all-reduce.7.cloned.1.call-done = (bf16[1,256,1536]{2,1,0:T(8,128)(2,1)}, bf16[1,256,1536]{2,1,0:T(8,128)(2,1)}, bf16[1,256,512]{2,1,0:T(8,128)(2,1)}, bf16[1,2...) async-done(((bf16[1,256,1536]{2,1,0:T(8,128)(2,1)}, ...) | async-done | bytes 6291472 | tf_op jit(solution)/shard_map/psum | solution.py:285
  873.6 7.7 multiply_subtract_fusion.2
  883.2 8.8 multiply_subtract_fusion.1
  892.6 6.2 multiply_subtract_fusion
  (461 shorter events, 181.2 us)
Async XLA Ops:
  7.2 62.5 %all-gather.21.cloned.1.call-start = ((), (), s32[]{:S(2)}) async-start(), calls=%async_computation.24 | async-start | bytes 2359296 | tf_op jit(solution)/shard_map/all_gather | solution.py:39
  10.6 139.6 %all-gather.23.cloned.1.call-start = ((), (), s32[]{:S(2)}) async-start(), calls=%async_computation.25 | async-start | bytes 3145728 | tf_op jit(solution)/shard_map/all_gather | solution.py:41
  14.6 144.9 %all-gather.25.cloned.1.call-start = ((), (), s32[]{:S(2)}) async-start(), calls=%async_computation.26 | async-start | bytes 3145728 | tf_op jit(solution)/shard_map/all_gather | solution.py:42
  17.1 14.8 %copy-start.68 = (f32[2,6,256]{2,0,1:T(2,128)S(1)}, f32[2,6,256]{2,0,1:T(2,128)}, u32[]{:S(2)}) copy-start(f32[2,6,256]{2,0,1:T(2,128)} %param.48) | copy-start | bytes 36868
  18.6 15.8 %copy-start.66 = (f32[2,8,169]{2,1,0:T(8,128)S(1)}, f32[2,8,169]{2,1,0:T(8,128)}, u32[]{:S(2)}) copy-start(f32[2,8,169]{2,1,0:T(8,128)} %param.45) | copy-start | bytes 32452
  18.6 21.3 %copy-start.55 = (s32[4,49,49]{2,0,1:T(4,128)S(1)}, s32[4,49,49]{2,0,1:T(4,128)}, u32[]{:S(2)}) copy-start(s32[4,49,49]{2,0,1:T(4,128)} %param.31) | copy-start | bytes 115252
  18.6 21.6 %copy-start.120 = (s32[49,49]{1,0:T(8,128)S(1)}, s32[49,49]{1,0:T(8,128)}, u32[]{:S(2)}) copy-start(s32[49,49]{1,0:T(8,128)} %param.32) | copy-start | bytes 28816
  18.6 159.6 %all-gather.27.cloned.1.call-start = ((), (), s32[]{:S(2)}) async-start(), calls=%async_computation.27 | async-start | bytes 2359296 | tf_op jit(solution)/shard_map/all_gather | solution.py:39
  19.2 238.9 %all-gather.29.cloned.1.call-start = ((), (), s32[]{:S(2)}) async-start(), calls=%async_computation.28 | async-start | bytes 3145728 | tf_op jit(solution)/shard_map/all_gather | solution.py:41
  19.3 24.6 %copy-start.31 = (f32[2,256,512]{2,1,0:T(8,128)S(1)}, f32[2,256,512]{2,1,0:T(8,128)}, u32[]{:S(2)}) copy-start(f32[2,256,512]{2,1,0:T(8,128)} %param.36) | copy-start | bytes 3145732
  19.8 247.4 %all-gather.31.cloned.1.call-start = ((), (), s32[]{:S(2)}) async-start(), calls=%async_computation.29 | async-start | bytes 3145728 | tf_op jit(solution)/shard_map/all_gather | solution.py:42
  20.4 562.4 %reduce-scatter.19.cloned.1.call-start = ((), (), s32[]{:S(2)}) async-start(), calls=%async_computation.15 | async-start | bytes 786432 | tf_op jit(solution)/shard_map/reduce_scatter | solution.py:264
  20.5 33.2 %copy-start.89 = (pred[196]{0:T(512)(128)(4,1)}, pred[196]{0:T(512)(128)(4,1)S(1)}, u32[]{:S(2)}) copy-start(pred[196]{0:T(512)(128)(4,1)S(1)} %compare_and_fusion.3) | copy-start | bytes 592
  23.7 145.6 %copy-start.100 = (pred[196]{0:T(512)(128)(4,1)}, pred[196]{0:T(512)(128)(4,1)S(1)}, u32[]{:S(2)}) copy-start(pred[196]{0:T(512)(128)(4,1)S(1)} %compare_and_fusion.2) | copy-start | bytes 592
  31.3 118.8 %copy-start.87 = (f32[1,2048]{1,0:T(1,128)}, f32[1,2048]{1,0:T(1,128)S(1)}, u32[]{:S(2)}) copy-start(f32[1,2048]{1,0:T(1,128)S(1)} %slice.264) | copy-start | bytes 24580
  32.0 134.7 %copy-start.85 = (s32[1024]{0:T(1024)}, s32[1024]{0:T(1024)S(1)}, u32[]{:S(2)}) copy-start(s32[1024]{0:T(1024)S(1)} %pad_clamp_fusion.2) | copy-start | bytes 12292
  32.0 19.0 %copy-start.86 = (s32[1024]{0:T(1024)}, s32[1024]{0:T(1024)S(1)}, u32[]{:S(2)}) copy-start(s32[1024]{0:T(1024)S(1)} %pad_clamp_fusion.3) | copy-start | bytes 12292
  34.4 143.8 %copy-start.109 = (f32[1,1,512]{2,0,1:T(1,128)}, f32[1,1,512]{2,0,1:T(1,128)S(1)}, u32[]{:S(2)}) copy-start(f32[1,1,512]{2,0,1:T(1,128)S(1)} %get-tuple-element.191) | copy-start | bytes 6148
  34.5 223.7 %copy-start.105 = (f32[1,1,512]{2,0,1:T(1,128)}, f32[1,1,512]{2,0,1:T(1,128)S(1)}, u32[]{:S(2)}) copy-start(f32[1,1,512]{2,0,1:T(1,128)S(1)} %get-tuple-element.188) | copy-start | bytes 6148
  34.5 249.0 %copy-start.75 = (f32[1,1,512]{2,0,1:T(1,128)}, f32[1,1,512]{2,0,1:T(1,128)S(1)}, u32[]{:S(2)}) copy-start(f32[1,1,512]{2,0,1:T(1,128)S(1)} %get-tuple-element.187) | copy-start | bytes 6148
  39.9 29.8 %copy-start.77 = (f32[1,1,512]{2,0,1:T(1,128)}, f32[1,1,512]{2,0,1:T(1,128)S(1)}, u32[]{:S(2)}) copy-start(f32[1,1,512]{2,0,1:T(1,128)S(1)} %get-tuple-element.198) | copy-start | bytes 6148
  39.9 29.8 %copy-start.107 = (f32[1,1,512]{2,0,1:T(1,128)}, f32[1,1,512]{2,0,1:T(1,128)S(1)}, u32[]{:S(2)}) copy-start(f32[1,1,512]{2,0,1:T(1,128)S(1)} %get-tuple-element.199) | copy-start | bytes 6148
  39.9 110.3 %copy-start.72 = (f32[1,1,512]{2,0,1:T(1,128)}, f32[1,1,512]{2,0,1:T(1,128)S(1)}, u32[]{:S(2)}) copy-start(f32[1,1,512]{2,0,1:T(1,128)S(1)} %get-tuple-element.195) | copy-start | bytes 6148
  39.9 110.3 %copy-start.103 = (f32[1,1,512]{2,0,1:T(1,128)}, f32[1,1,512]{2,0,1:T(1,128)S(1)}, u32[]{:S(2)}) copy-start(f32[1,1,512]{2,0,1:T(1,128)S(1)} %get-tuple-element.196) | copy-start | bytes 6148
  57.3 88.4 %copy-start.2 = (f32[196,6,512]{2,0,1:T(8,128)}, f32[196,6,512]{2,0,1:T(8,128)S(1)}, u32[]{:S(2)}) copy-start(f32[196,6,512]{2,0,1:T(8,128)S(1)} %get-tuple-element.169) | copy-start | bytes 7225348
  57.3 12.4 %copy-start.53 = (f32[6,196]{1,0:T(8,128)}, f32[6,196]{1,0:T(8,128)S(1)}, u32[]{:S(2)}) copy-start(f32[6,196]{1,0:T(8,128)S(1)} %broadcast_multiply_fusion.3) | copy-start | bytes 14116
  57.9 11.8 %copy-start.64 = (f32[6,196]{1,0:T(8,128)}, f32[6,196]{1,0:T(8,128)S(1)}, u32[]{:S(2)}) copy-start(f32[6,196]{1,0:T(8,128)S(1)} %fusion.113) | copy-start | bytes 14116
  148.2 11.3 %copy-start.49 = (f32[6,196]{1,0:T(8,128)}, f32[6,196]{1,0:T(8,128)S(1)}, u32[]{:S(2)}) copy-start(f32[6,196]{1,0:T(8,128)S(1)} %broadcast_multiply_fusion.2) | copy-start | bytes 14116
  256.1 27.3 %copy-start.51 = (f32[6,196]{1,0:T(8,128)}, f32[6,196]{1,0:T(8,128)S(1)}, u32[]{:S(2)}) copy-start(f32[6,196]{1,0:T(8,128)S(1)} %broadcast_multiply_fusion) | copy-start | bytes 14116
  258.1 25.3 %copy-start.58 = (f32[6,196]{1,0:T(8,128)}, f32[6,196]{1,0:T(8,128)S(1)}, u32[]{:S(2)}) copy-start(f32[6,196]{1,0:T(8,128)S(1)} %fusion.116) | copy-start | bytes 14116
  341.5 241.2 %reduce-scatter.17.cloned.1.call-start = ((), (), s32[]{:S(2)}) async-start(), calls=%async_computation.14 | async-start | bytes 786432 | tf_op jit(solution)/shard_map/reduce_scatter | solution.py:264
  406.5 10.8 %copy-start.43 = (bf16[6,196,512]{2,1,0:T(8,128)(2,1)}, bf16[6,196,512]{2,1,0:T(8,128)(2,1)S(1)}, u32[]{:S(2)}) copy-start(bf16[6,196,512]{2,1,0:T(8,128)(2,1)S(1)} %get-tuple-element.143) | copy-start | bytes 3612676
  406.5 10.8 %copy-start.8 = (f32[6,196,512]{2,1,0:T(8,128)S(1)}, f32[6,196,512]{2,1,0:T(8,128)}, u32[]{:S(2)}) copy-start(f32[6,196,512]{2,1,0:T(8,128)} %copy-done.6) | copy-start | bytes 7225348
  406.5 10.8 %copy-start.50 = (f32[6,196]{1,0:T(8,128)S(1)}, f32[6,196]{1,0:T(8,128)}, u32[]{:S(2)}) copy-start(f32[6,196]{1,0:T(8,128)} %copy-done.49) | copy-start | bytes 14116
  435.5 147.3 %reduce-scatter.15.cloned.1.call-start = ((), (), s32[]{:S(2)}) async-start(), calls=%async_computation.13 | async-start | bytes 2359296 | tf_op jit(solution)/shard_map/reduce_scatter | solution.py:261
  462.4 120.4 %reduce-scatter.13.cloned.1.call-start = ((), (), s32[]{:S(2)}) async-start(), calls=%async_computation.12 | async-start | bytes 2359296 | tf_op jit(solution)/shard_map/reduce_scatter | solution.py:261
  472.3 12.4 %slice-start = ((s8[11010048]{0:T(1024)(128)(4,1)}), s8[4194304]{0:T(1024)(128)(4,1)S(1)}, s32[]{:S(2)}) async-start(s8[11010048]{0:T(1024)(128)(4,1)} %bitcast.331), calls=%async_computation.31 | async-start | bytes 8388608
  472.3 12.4 %slice-start.1 = ((s8[11010048]{0:T(1024)(128)(4,1)}), s8[4194304]{0:T(1024)(128)(4,1)S(1)}, s32[]{:S(2)}) async-start(s8[11010048]{0:T(1024)(128)(4,1)} %bitcast.331), calls=%async_computation.32 | async-start | bytes 8388608
  513.2 13.8 %copy-start.3 = (f32[196,6,512]{2,0,1:T(8,128)S(1)}, f32[196,6,512]{2,0,1:T(8,128)}, u32[]{:S(2)}) copy-start(f32[196,6,512]{2,0,1:T(8,128)} %copy-done.2) | copy-start | bytes 7225348
  513.2 13.8 %copy-start.54 = (f32[6,196]{1,0:T(8,128)S(1)}, f32[6,196]{1,0:T(8,128)}, u32[]{:S(2)}) copy-start(f32[6,196]{1,0:T(8,128)} %copy-done.53) | copy-start | bytes 14116
  513.2 13.8 %copy-start.65 = (f32[6,196]{1,0:T(8,128)S(1)}, f32[6,196]{1,0:T(8,128)}, u32[]{:S(2)}) copy-start(f32[6,196]{1,0:T(8,128)} %copy-done.64) | copy-start | bytes 14116
  513.2 13.8 %copy-start.78 = (f32[1,1,512]{2,0,1:T(1,128)S(1)}, f32[1,1,512]{2,0,1:T(1,128)}, u32[]{:S(2)}) copy-start(f32[1,1,512]{2,0,1:T(1,128)} %copy-done.77) | copy-start | bytes 6148
  513.2 13.8 %copy-start.108 = (f32[1,1,512]{2,0,1:T(1,128)S(1)}, f32[1,1,512]{2,0,1:T(1,128)}, u32[]{:S(2)}) copy-start(f32[1,1,512]{2,0,1:T(1,128)} %copy-done.107) | copy-start | bytes 6148
  533.7 49.1 %reduce-scatter.27.cloned.1.call-start = ((), (), s32[]{:S(2)}) async-start(), calls=%async_computation.19 | async-start | bytes 3145728 | tf_op jit(solution)/shard_map/reduce_scatter | solution.py:270
  540.8 42.0 %reduce-scatter.23.cloned.1.call-start = ((), (), s32[]{:S(2)}) async-start(), calls=%async_computation.17 | async-start | bytes 3145728 | tf_op jit(solution)/shard_map/reduce_scatter | solution.py:267
  549.1 37.6 %reduce-scatter.25.cloned.1.call-start = ((), (), s32[]{:S(2)}) async-start(), calls=%async_computation.18 | async-start | bytes 3145728 | tf_op jit(solution)/shard_map/reduce_scatter | solution.py:270
  556.6 43.7 %reduce-scatter.21.cloned.1.call-start = ((), (), s32[]{:S(2)}) async-start(), calls=%async_computation.16 | async-start | bytes 3145728 | tf_op jit(solution)/shard_map/reduce_scatter | solution.py:267
  564.7 73.3 %reduce-scatter.31.cloned.1.call-start = ((), (), s32[]{:S(2)}) async-start(), calls=%async_computation.21 | async-start | bytes 12288 | tf_op jit(solution)/shard_map/reduce_scatter | solution.py:273
  568.8 69.2 %reduce-scatter.29.cloned.1.call-start = ((), (), s32[]{:S(2)}) async-start(), calls=%async_computation.20 | async-start | bytes 12288 | tf_op jit(solution)/shard_map/reduce_scatter | solution.py:273
  570.6 67.3 %reduce-scatter.35.cloned.1.call-start = ((), (), s32[]{:S(2)}) async-start(), calls=%async_computation.23 | async-start | bytes 12288 | tf_op jit(solution)/shard_map/reduce_scatter | solution.py:276
  579.2 65.9 %reduce-scatter.33.cloned.1.call-start = ((), (), s32[]{:S(2)}) async-start(), calls=%async_computation.22 | async-start | bytes 12288 | tf_op jit(solution)/shard_map/reduce_scatter | solution.py:276
  582.5 287.0 %all-reduce.7.cloned.1.call-start = ((), (), s32[]{:S(2)}) async-start(), calls=%async_computation.30 | async-start | bytes 12582912 | tf_op jit(solution)/shard_map/psum | solution.py:285
  635.0 90.9 %copy-start.69 = (f32[2,6,256]{2,0,1:T(2,128)S(1)}, f32[2,6,256]{2,0,1:T(2,128)}, u32[]{:S(2)}) copy-start(f32[2,6,256]{2,0,1:T(2,128)} %param.48) | copy-start | bytes 36868
  635.0 90.9 %copy-start.81 = (f32[2,6,256]{2,0,1:T(2,128)S(1)}, f32[2,6,256]{2,0,1:T(2,128)}, u32[]{:S(2)}) copy-start(f32[2,6,256]{2,0,1:T(2,128)} %param.50) | copy-start | bytes 36868
  635.0 90.9 %copy-start.82 = (f32[2,6,256]{2,0,1:T(2,128)S(1)}, f32[2,6,256]{2,0,1:T(2,128)}, u32[]{:S(2)}) copy-start(f32[2,6,256]{2,0,1:T(2,128)} %param.49) | copy-start | bytes 36868
  635.0 92.7 %copy-start.67 = (f32[2,8,169]{2,1,0:T(8,128)S(1)}, f32[2,8,169]{2,1,0:T(8,128)}, u32[]{:S(2)}) copy-start(f32[2,8,169]{2,1,0:T(8,128)} %param.45) | copy-start | bytes 32452
  635.0 92.7 %copy-start.79 = (f32[2,8,169]{2,1,0:T(8,128)S(1)}, f32[2,8,169]{2,1,0:T(8,128)}, u32[]{:S(2)}) copy-start(f32[2,8,169]{2,1,0:T(8,128)} %param.47) | copy-start | bytes 32452
  635.0 92.7 %copy-start.80 = (f32[2,8,169]{2,1,0:T(8,128)S(1)}, f32[2,8,169]{2,1,0:T(8,128)}, u32[]{:S(2)}) copy-start(f32[2,8,169]{2,1,0:T(8,128)} %param.46) | copy-start | bytes 32452
  635.0 93.3 %copy-start.71 = (f32[2,1536]{1,0:T(2,128)S(1)}, f32[2,1536]{1,0:T(2,128)}, u32[]{:S(2)}) copy-start(f32[2,1536]{1,0:T(2,128)} %param.51) | copy-start | bytes 36868
  635.0 93.3 %copy-start.83 = (f32[2,1536]{1,0:T(2,128)S(1)}, f32[2,1536]{1,0:T(2,128)}, u32[]{:S(2)}) copy-start(f32[2,1536]{1,0:T(2,128)} %param.53) | copy-start | bytes 36868
  635.1 93.3 %copy-start.84 = (f32[2,1536]{1,0:T(2,128)S(1)}, f32[2,1536]{1,0:T(2,128)}, u32[]{:S(2)}) copy-start(f32[2,1536]{1,0:T(2,128)} %param.52) | copy-start | bytes 36868
  635.1 234.4 %copy-start.32 = (f32[2,256,512]{2,1,0:T(8,128)S(1)}, f32[2,256,512]{2,1,0:T(8,128)}, u32[]{:S(2)}) copy-start(f32[2,256,512]{2,1,0:T(8,128)} %param.36) | copy-start | bytes 3145732
  635.1 234.4 %copy-start.44 = (f32[2,256,512]{2,1,0:T(8,128)S(1)}, f32[2,256,512]{2,1,0:T(8,128)}, u32[]{:S(2)}) copy-start(f32[2,256,512]{2,1,0:T(8,128)} %param.38) | copy-start | bytes 3145732
  635.1 234.4 %copy-start.45 = (f32[2,256,512]{2,1,0:T(8,128)S(1)}, f32[2,256,512]{2,1,0:T(8,128)}, u32[]{:S(2)}) copy-start(f32[2,256,512]{2,1,0:T(8,128)} %param.37) | copy-start | bytes 3145732
  (83 other events, 488.4 us)
Sparse Core Ops, SparseCore 0:
  10.7 12.4 all-gather.20
  25.4 12.1 all-gather.22
  39.7 11.7 all-gather.24
  53.4 11.3 all-gather.26
  66.7 11.7 all-gather.28
  80.5 11.7 all-gather.30
  341.6 10.6 reduce-scatter.18
  435.6 10.6 reduce-scatter.16
  462.6 11.7 reduce-scatter.14
  533.8 11.8 reduce-scatter.12
  548.6 10.7 reduce-scatter.26
  562.1 10.9 reduce-scatter.22
  575.9 10.6 reduce-scatter.24
  589.4 10.7 reduce-scatter.20
  602.9 8.5 reduce-scatter.30
  614.1 8.5 reduce-scatter.28
  625.3 8.5 reduce-scatter.34
  636.5 8.5 reduce-scatter.32
  651.5 217.9 all-reduce.6
where the time goes:
time: 913 us; the launch traced here: 906 us
  local copies, waits for them, and re-layouts  261 us (29%)
  matrix products  223 us (24%)
  waiting for transfers between devices  167 us (18%)
  other arithmetic  137 us (15%)
  blocking collectives  100 us (11%)
  between operations  16.5 us (2%)
    psum x1, waiting for transfers between devices, shards(): lax.psum(o_attend.astype(jnp.bfloat16), 'rep').astype(jnp.float32)  140 us
    psum x1, blocking collectives, shards(): lax.psum(o_table.astype(jnp.bfloat16), 'rep').astype(jnp.float32)  80.8 us
    unnamed x270, local copies, waits for them, and re-layouts  63.7 us
    dot_general x8, matrix products, matmul_back(): jnp.einsum('btn,in->bti', left, right, preferred_element_type=jnp.float32)  49.3 us
    dot_general x8, matrix products, weight_grad(): jnp.einsum('bti,btn->in', left, right, preferred_element_type=jnp.float32)  46.9 us
    dot_general x8, matrix products, matmul(): jnp.einsum('bti,in->btn', left, right, preferred_element_type=jnp.float32)  46.1 us
    sub x7, other arithmetic, adam(): weight - rate * (first_hat / (jnp.sqrt(second_hat) + 1e-08) + decay * wei...  27.5 us
    convert_element_type x2, local copies, waits for them, and re-layouts, backward_layer(): grad_lifted.reshape(count, tokens, 3 * width).astype(jnp.bfloat16)  27.1 us
  transfers between devices with their start and end apart: 19, of which 4 were waited for; matrix products, arithmetic and copies ran while one was open for 56% of the time, Pallas kernels for 0%

commit v1 on v0

v1 whole, which is shorter than its diff:
```python
import jax
import jax.numpy as jnp
from jax import lax
from jax.experimental import pallas as pl
from jax.experimental.pallas import tpu as pltpu
from jax.sharding import PartitionSpec as P

D = 512
FF = 2048
STEP = 10
DEPTH = 32
LANES = 128
PACK = LANES // DEPTH
ROWS = 112
SCALE = DEPTH ** (-0.5)
BF = jnp.bfloat16
F32 = jnp.float32


def dot(left, right, dims):
    return lax.dot_general(left, right, (dims, ((), ())), preferred_element_type=F32)


def mm(left, right):
    return dot(left, right, ((1,), (0,)))


def mm_t(left, right):
    return dot(left, right, ((1,), (1,)))


def t_mm(left, right):
    return dot(left, right, ((0,), (0,)))


def head_masks():
    lane = lax.broadcasted_iota(jnp.int32, (1, LANES), 1)
    return [(lane // DEPTH == h) for h in range(PACK)]


def stack_heads(x, masks):
    return jnp.concatenate([x * m.astype(F32).astype(BF) for m in masks], axis=0)


def pad_keys(x):
    return jnp.concatenate([x, jnp.zeros((LANES - ROWS, LANES), x.dtype)], axis=0)


def pick_heads(x, masks):
    out = x[0:ROWS]
    for h in range(1, PACK):
        out = jnp.where(masks[h], x[h * ROWS : (h + 1) * ROWS], out)
    return out


def softmax_rows(s):
    e = jnp.exp(s - jnp.max(s, axis=-1, keepdims=True))
    return e * (1.0 / jnp.sum(e, axis=-1, keepdims=True))


def attend_fwd_kernel(c_ref, bias_ref, a_ref):
    masks = head_masks()
    width = a_ref.shape[1]
    for g in range(width // LANES):
        col = g * LANES
        q = c_ref[:, col : col + LANES]
        k = pad_keys(c_ref[:, width + col : width + col + LANES])
        v = pad_keys(c_ref[:, 2 * width + col : 2 * width + col + LANES])
        s = mm_t(stack_heads(q, masks), k) * SCALE
        s = s + bias_ref[0, g * PACK * ROWS : (g + 1) * PACK * ROWS, :]
        p = softmax_rows(s).astype(BF)
        a_ref[:, col : col + LANES] = pick_heads(mm(p, v), masks).astype(BF)


def attend_bwd_kernel(c_ref, da_ref, bias_ref, dc_ref, z_ref):
    masks = head_masks()
    width = da_ref.shape[1]

    @pl.when((pl.program_id(0) == 0) & (pl.program_id(1) == 0))
    def _():
        z_ref[...] = jnp.zeros_like(z_ref)

    for g in range(width // LANES):
        col = g * LANES
        rows = slice(g * PACK * ROWS, (g + 1) * PACK * ROWS)
        q = c_ref[:, col : col + LANES]
        k = pad_keys(c_ref[:, width + col : width + col + LANES])
        v = pad_keys(c_ref[:, 2 * width + col : 2 * width + col + LANES])
        qs = stack_heads(q, masks)
        ds = stack_heads(da_ref[:, col : col + LANES], masks)
        p = softmax_rows(mm_t(qs, k) * SCALE + bias_ref[0, rows, :])
        dp = mm_t(ds, v)
        inner = jnp.sum(p * dp, axis=-1, keepdims=True)
        dz = (p * (dp - inner)).astype(BF)
        z_ref[rows, :] += dz.astype(F32)
        dv = t_mm(p.astype(BF), ds)
        dk = t_mm(dz, qs) * SCALE
        dq = pick_heads(mm(dz, k), masks) * SCALE
        dc_ref[:, col : col + LANES] = dq.astype(BF)
        dc_ref[:, width + col : width + col + LANES] = dk[:ROWS].astype(BF)
        dc_ref[:, 2 * width + col : 2 * width + col + LANES] = dv[:ROWS].astype(BF)


def attend_fwd(c, bias):
    pairs, stacked, _ = bias.shape
    images = c.shape[0] // (pairs * ROWS)
    width = c.shape[1] // 3
    row = lambda t, b: (b * pairs + t, 0)
    return pl.pallas_call(
        attend_fwd_kernel,
        grid=(pairs, images),
        in_specs=[
            pl.BlockSpec((ROWS, 3 * width), row),
            pl.BlockSpec((1, stacked, LANES), lambda t, b: (t, 0, 0)),
        ],
        out_specs=pl.BlockSpec((ROWS, width), row),
        out_shape=jax.ShapeDtypeStruct((c.shape[0], width), BF),
        compiler_params=pltpu.CompilerParams(vmem_limit_bytes=32 * 1024 * 1024),
        cost_estimate=pl.CostEstimate(
            flops=4 * pairs * images * stacked * LANES * LANES,
            bytes_accessed=c.size * 3 + bias.size * 4,
            transcendentals=pairs * images * stacked * LANES,
        ),
    )(c, bias)


def attend_bwd(c, da, bias):
    pairs, stacked, _ = bias.shape
    images = c.shape[0] // (pairs * ROWS)
    width = c.shape[1] // 3
    row = lambda t, b: (b * pairs + t, 0)
    return pl.pallas_call(
        attend_bwd_kernel,
        grid=(pairs, images),
        in_specs=[
            pl.BlockSpec((ROWS, 3 * width), row),
            pl.BlockSpec((ROWS, width), row),
            pl.BlockSpec((1, stacked, LANES), lambda t, b: (t, 0, 0)),
        ],
        out_specs=[
            pl.BlockSpec((ROWS, 3 * width), row),
            pl.BlockSpec((stacked, LANES), lambda t, b: (0, 0)),
        ],
        out_shape=[
            jax.ShapeDtypeStruct(c.shape, BF),
            jax.ShapeDtypeStruct((stacked, LANES), F32),
        ],
        compiler_params=pltpu.CompilerParams(vmem_limit_bytes=32 * 1024 * 1024),
        cost_estimate=pl.CostEstimate(
            flops=10 * pairs * images * stacked * LANES * LANES,
            bytes_accessed=c.size * 5 + bias.size * 4,
            transcendentals=pairs * images * stacked * LANES,
        ),
    )(c, da, bias)


def row_stats(v):
    mean = jnp.mean(v, axis=-1, keepdims=True)
    centered = v - mean
    rstd = lax.rsqrt(jnp.mean(centered * centered, axis=-1, keepdims=True) + 1e-05)
    return mean, rstd


def norm_rows(v, gain, shift):
    mean, rstd = row_stats(v)
    return ((v - mean) * rstd * gain + shift).astype(BF), (mean, rstd)


def norm_back(v, stats, gain, do):
    mean, rstd = stats
    r = (v - mean) * rstd
    dg = do * gain
    grad = (
        dg - jnp.mean(dg, axis=-1, keepdims=True) - r * jnp.mean(dg * r, axis=-1, keepdims=True)
    ) * rstd
    return grad, jnp.sum(do * r, axis=0), jnp.sum(do, axis=0)


def gelu_both(f):
    cdf = 0.5 * (1.0 + lax.erf(f * 0.7071067811865476))
    slope = cdf + f * jnp.exp(-0.5 * f * f) * 0.3989422804014327
    return (f * cdf).astype(BF), slope.astype(BF)


def relative_table(rel_index, rows):
    return (rel_index[:, :, None] == jnp.arange(rows, dtype=jnp.int32)[None, None, :]).astype(F32)


def pair_bias(table, onehot, penalty):
    position = jnp.einsum("hr,ijr->hij", table.astype(F32), onehot, precision=lax.Precision.HIGHEST)
    size = position.shape[-1]
    both = position[None, None] + penalty.reshape(-1, 2, 1, size, size)
    first = jnp.pad(
        both[:, 0], ((0, 0), (0, 0), (0, ROWS - size), (0, LANES - size)), constant_values=-1e30
    )
    second = jnp.pad(
        both[:, 1],
        ((0, 0), (0, 0), (size, ROWS - 2 * size), (size, LANES - 2 * size)),
        constant_values=-1e30,
    )
    row = lax.broadcasted_iota(jnp.int32, (ROWS, LANES), 0)
    lane = lax.broadcasted_iota(jnp.int32, (ROWS, LANES), 1)
    both = jnp.maximum(first, second)
    both = jnp.where((row >= 2 * size) & (lane < size), 0.0, both)
    return both.reshape(penalty.shape[0] // 2, -1, LANES)


def padded_order(order, windows):
    pairs = order.reshape(windows // 2, -1)
    return jnp.pad(pairs, ((0, 0), (0, ROWS - pairs.shape[1])), constant_values=-1).reshape(-1)


def place(onehot, x, contract):
    count = x.shape[0]
    hot = jnp.broadcast_to(onehot[None], (count,) + onehot.shape)
    return lax.dot_general(
        hot, x, (((contract + 1,), (1,)), ((0,), (0,))), preferred_element_type=F32
    )


def forward_layer(s, bias, weights):
    attend, output, expand, shrink, gains, offsets = weights
    width = attend.shape[0]
    qkv_bias = jnp.concatenate(
        [offsets[:width], jnp.zeros((width,), F32), offsets[width : 2 * width]]
    )
    wide = s.astype(F32)
    u, stats_one = norm_rows(wide, gains[0], gains[1])
    c = (mm(u, attend) + qkv_bias).astype(BF)
    a = attend_fwd(c, bias)
    m = wide + mm(a, output) + gains[2]
    n, stats_two = norm_rows(m, gains[3], gains[4])
    e, slope = gelu_both(mm(n, expand) + offsets[2 * width :])
    out = (m + mm(e, shrink) + gains[5]).astype(BF)
    return out, (s, u, stats_one, c, a, m, n, stats_two, e, slope)


def backward_layer(gs, bias, weights, saved, send):
    attend, output, expand, shrink, gains, offsets = weights
    s, u, stats_one, c, a, m, n, stats_two, e, slope = saved
    dy = gs.astype(BF)
    wide = gs.astype(F32)
    grad_last = jnp.sum(dy.astype(F32), axis=0)
    grad_shrink = t_mm(e, dy).astype(BF)
    df = (mm_t(dy, shrink) * slope.astype(F32)).astype(BF)
    grad_fbias = jnp.sum(df.astype(F32), axis=0)
    grad_expand = t_mm(n, df).astype(BF)
    df, grad_shrink, grad_expand = lax.optimization_barrier((df, grad_shrink, grad_expand))
    ffn = send((grad_expand, grad_shrink))
    dn = mm_t(df, expand)
    dm, grad_gain_two, grad_shift_two = norm_back(m, stats_two, gains[3], dn)
    dm = dm + wide
    dq_m = dm.astype(BF)
    grad_pbias = jnp.sum(dq_m.astype(F32), axis=0)
    grad_output = t_mm(a, dq_m).astype(BF)
    da = mm_t(dq_m, output).astype(BF)
    dc, z = attend_bwd(c, da, bias)
    width = attend.shape[0]
    sums = jnp.sum(dc.astype(F32), axis=0)
    grad_attend = t_mm(u, dc).astype(BF)
    dc, grad_attend, grad_output = lax.optimization_barrier((dc, grad_attend, grad_output))
    att = send((grad_attend, grad_output))
    du = mm_t(dc, attend)
    g, grad_gain_one, grad_shift_one = norm_back(s.astype(F32), stats_one, gains[0], du)
    g = (g + dm).astype(BF)
    grad_vectors = jnp.stack(
        [grad_gain_one, grad_shift_one, grad_pbias, grad_gain_two, grad_shift_two, grad_last]
    )
    grad_biases = jnp.concatenate([sums[:width], sums[2 * width :], grad_fbias])
    return g, (att, ffn), (z, grad_vectors, grad_biases)


class Sender:
    def __init__(self):
        self.last = None

    def __call__(self, grads):
        owned = tuple(
            lax.psum_scatter(g, "shard", scatter_dimension=0, tiled=True) for g in grads
        )
        if self.last is not None:
            owned, self.last = lax.optimization_barrier((owned, self.last))
        self.last = lax.psum(owned, "rep")
        return self.last


def adam(weight, moment, square, grad, rate, decay):
    moment_new = 0.9 * moment + 0.1 * grad
    square_new = 0.999 * square + 0.001 * grad * grad
    first_hat = moment_new / (1.0 - 0.9**STEP)
    second_hat = square_new / (1.0 - 0.999**STEP)
    weight_new = weight - rate * (first_hat / (jnp.sqrt(second_hat) + 1e-08) + decay * weight)
    return (moment_new, square_new, weight_new)


def shards(
    images,
    cotangent,
    window_map,
    shift_mask,
    rel_index,
    attend_weight,
    attend_moment,
    attend_square,
    output_weight,
    output_moment,
    output_square,
    expand_weight,
    expand_moment,
    expand_square,
    reduce_weight,
    reduce_moment,
    reduce_square,
    bias_table,
    table_moment,
    table_square,
    layer_vectors,
    vector_moment,
    vector_square,
    wide_bias,
    biases_moment,
    biases_square,
):
    layers = attend_weight.shape[0]
    windows = shift_mask.shape[0]
    count, tokens, width = images.shape
    ranks = lax.axis_size("shard")

    small = jnp.concatenate(
        [item.astype(BF).reshape(-1) for item in (layer_vectors, wide_bias, bias_table)]
    )
    small = lax.all_gather(small, "shard", axis=0)
    cut_one = layer_vectors.size
    cut_two = cut_one + wide_bias.size
    vectors = small[:, :cut_one].reshape((ranks,) + layer_vectors.shape)
    vectors = vectors.transpose(1, 2, 0, 3).reshape(layers, 6, width).astype(F32)
    biases = small[:, cut_one:cut_two].reshape((ranks,) + wide_bias.shape)
    biases = biases.transpose(1, 0, 2).reshape(layers, -1).astype(F32)
    table = small[:, cut_two:].reshape((ranks,) + bias_table.shape)
    table = table.transpose(1, 0, 2, 3).reshape(layers, -1, bias_table.shape[2])

    weights = []
    for layer in range(layers):
        mats = tuple(
            lax.all_gather(item[layer].astype(BF), "shard", axis=0, tiled=True)
            for item in (attend_weight, output_weight, expand_weight, reduce_weight)
        )
        weights.append(mats + (vectors[layer], biases[layer]))

    mask_term = -100.0 * shift_mask.astype(F32)
    onehot = relative_table(rel_index, table.shape[2])
    bias = [
        pair_bias(table[layer], onehot, mask_term * float(layer % 2)) for layer in range(layers)
    ]
    orders = [padded_order(window_map[layer], windows) for layer in range(layers)]
    slots = orders[0].shape[0]
    token_ids = jnp.arange(tokens, dtype=jnp.int32)
    to_slots = [(o[:, None] == token_ids[None, :]).astype(BF) for o in orders]
    moves = [
        ((orders[l + 1][:, None] == orders[l][None, :]) & (orders[l + 1][:, None] >= 0)).astype(BF)
        for l in range(layers - 1)
    ]

    flat = lambda x: x.astype(BF).reshape(count * slots, width)
    split = lambda x: x.reshape(count, slots, width)
    state = flat(place(to_slots[0], images, 1))
    saved_all = []
    for layer in range(layers):
        out, saved = forward_layer(state, bias[layer], weights[layer])
        saved_all.append(saved)
        if layer + 1 < layers:
            state = flat(place(moves[layer], split(out), 1))
    block_out = place(to_slots[-1], split(out), 0).astype(BF)

    send = Sender()
    g = flat(place(to_slots[-1], cotangent, 1))
    sent = [None] * layers
    little = [None] * layers
    for layer in reversed(range(layers)):
        g, sent[layer], little[layer] = backward_layer(
            g, bias[layer], weights[layer], saved_all[layer], send
        )
        if layer > 0:
            g = flat(place(moves[layer - 1], split(g), 0))
    grad_state = place(to_slots[0], split(g), 0)

    size = rel_index.shape[0]
    z = jnp.stack([item[0] for item in little]).reshape(layers, -1, ROWS, LANES)
    z = z[:, :, :size, :size] + z[:, :, size : 2 * size, size : 2 * size]
    g_table = jnp.einsum("lhij,ijr->lhr", z, onehot, precision=lax.Precision.HIGHEST)
    g_vectors = jnp.stack([item[1] for item in little])
    g_biases = jnp.stack([item[2] for item in little])
    g_small = jnp.concatenate(
        [
            g_vectors.reshape(layers, 6, ranks, -1).transpose(2, 0, 1, 3).reshape(ranks, -1),
            g_biases.reshape(layers, ranks, -1).transpose(1, 0, 2).reshape(ranks, -1),
            g_table.reshape(layers, ranks, -1).transpose(1, 0, 2).reshape(ranks, -1),
        ],
        axis=1,
    )
    g_small = lax.psum(g_small, ("rep", "shard"))
    g_small = lax.dynamic_index_in_dim(g_small, lax.axis_index("shard"), 0, keepdims=False)
    own = lambda index, which: jnp.stack([sent[l][index][which] for l in range(layers)]).astype(F32)
    stacked = (
        own(0, 0),
        own(0, 1),
        own(1, 0),
        own(1, 1),
        g_small[cut_two:].reshape(bias_table.shape),
        g_small[:cut_one].reshape(layer_vectors.shape),
        g_small[cut_one:cut_two].reshape(wide_bias.shape),
    )
    ma, sa, wa = adam(
        attend_weight, attend_moment, attend_square, stacked[0], 3.0 * D ** (-0.5), 0.05
    )
    mo, so, wo = adam(
        output_weight, output_moment, output_square, stacked[1], 3.0 * (8.0 / D) ** 0.5, 0.05
    )
    me, se, we = adam(
        expand_weight, expand_moment, expand_square, stacked[2], 3.0 * D ** (-0.5), 0.05
    )
    mr, sr, wr = adam(
        reduce_weight, reduce_moment, reduce_square, stacked[3], 3.0 * FF ** (-0.5), 0.05
    )
    mt, st, wt = adam(bias_table, table_moment, table_square, stacked[4], 3.0, 0.0)
    mv, sv, wv = adam(layer_vectors, vector_moment, vector_square, stacked[5], 1.0, 0.0)
    mb, sb, wb = adam(wide_bias, biases_moment, biases_square, stacked[6], 1.5, 0.0)
    return (
        block_out,
        grad_state,
        ma,
        sa,
        wa,
        mo,
        so,
        wo,
        me,
        se,
        we,
        mr,
        sr,
        wr,
        mt,
        st,
        wt,
        mv,
        sv,
        wv,
        mb,
        sb,
        wb,
    )


def solution(mesh):
    return jax.shard_map(
        shards,
        mesh=mesh,
        in_specs=(
            P(("rep", "shard"), None, None),
            P(("rep", "shard"), None, None),
            P(),
            P(),
            P(),
            P(None, "shard", None),
            P(None, "shard", None),
            P(None, "shard", None),
            P(None, "shard", None),
            P(None, "shard", None),
            P(None, "shard", None),
            P(None, "shard", None),
            P(None, "shard", None),
            P(None, "shard", None),
            P(None, "shard", None),
            P(None, "shard", None),
            P(None, "shard", None),
            P(None, "shard", None),
            P(None, "shard", None),
            P(None, "shard", None),
            P(None, None, "shard"),
            P(None, None, "shard"),
            P(None, None, "shard"),
            P(None, "shard"),
            P(None, "shard"),
            P(None, "shard"),
        ),
        out_specs=(
            P(("rep", "shard"), None, None),
            P(("rep", "shard"), None, None),
            P(None, "shard", None),
            P(None, "shard", None),
            P(None, "shard", None),
            P(None, "shard", None),
            P(None, "shard", None),
            P(None, "shard", None),
            P(None, "shard", None),
            P(None, "shard", None),
            P(None, "shard", None),
            P(None, "shard", None),
            P(None, "shard", None),
            P(None, "shard", None),
            P(None, "shard", None),
            P(None, "shard", None),
            P(None, "shard", None),
            P(None, None, "shard"),
            P(None, None, "shard"),
            P(None, None, "shard"),
            P(None, "shard"),
            P(None, "shard"),
            P(None, "shard"),
        ),
        check_vma=False,
    )
```

time: 913 us -> 932 us (1.021)
  waiting for transfers between devices: 167 us -> 555 us
  local copies, waits for them, and re-layouts: 261 us -> 38.9 us
  blocking collectives: 100 us -> 8.28 us
  Pallas kernels: 0 us -> 88 us
  other arithmetic: 137 us -> 61.6 us
  matrix products: 223 us -> 154 us
    psum x1 -> x5, waiting for transfers between devices: 140 us -> 516 us  [the longest x4 397 us: __call__(): self.last = lax.psum(owned, 'rep')]
    pallas_call x0 -> x4, Pallas kernels: none -> 88 us  [the longest x2 61.4 us: attend_bwd(): pl.pallas_call(attend_bwd_kernel, grid=(pairs, images), in_specs=[pl.Bloc...]
    psum x1 -> x0, blocking collectives: 80.8 us -> none  [shards(): lax.psum(o_table.astype(jnp.bfloat16), 'rep').astype(jnp.float32)]
    dot_general x40 -> x33, matrix products: 223 us -> 154 us  [the longest x24 142 us: dot(): lax.dot_general(left, right, (dims, ((), ())), preferred_element_type=F32)]
    convert_element_type x8 -> x5, local copies, waits for them, and re-layouts: 53.6 us -> 0.12 us  [the longest x3 0.08 us: shards(): vectors.transpose(1, 2, 0, 3).reshape(layers, 6, width).astype(F32)]
    reduce_sum x20 -> x8, other arithmetic: 63.2 us -> 10.2 us  [the longest x4 3.78 us: row_stats(): jnp.mean(centered * centered, axis=-1, keepdims=True) + 1e-05]
    reshape x6 -> x11, local copies, waits for them, and re-layouts: 48.3 us -> 0.59 us  [the longest x3 0.21 us: shards(): g_table.reshape(layers, ranks, -1).transpose(1, 0, 2).reshape(ranks, -1)]
    unnamed x270 -> x186, local copies, waits for them, and re-layouts: 63.7 us -> 28.8 us
  transfers between devices with their start and end apart: 19 -> 19, of which waited for: 4 -> 9; matrix products, arithmetic and copies ran while one was open for 56% -> 21% of each run, Pallas kernels for 0% -> 10%
where the time goes in v1:
time: 932 us; the launch traced here: 924 us
  waiting for transfers between devices  555 us (60%)
  matrix products  154 us (17%)
  Pallas kernels  88 us (9%)
  other arithmetic  61.6 us (7%)
  local copies, waits for them, and re-layouts  38.9 us (4%)
  between operations  16.6 us (2%)
    psum x4, waiting for transfers between devices, __call__(): self.last = lax.psum(owned, 'rep')  397 us
    dot_general x24, matrix products, dot(): lax.dot_general(left, right, (dims, ((), ())), preferred_element_type=F32)  142 us
    psum x1, waiting for transfers between devices, shards(): g_small = lax.psum(g_small, ('rep', 'shard'))  119 us
    pallas_call x2, Pallas kernels, attend_bwd(): pl.pallas_call(attend_bwd_kernel, grid=(pairs, images), in_specs=[pl.Bloc...  61.4 us
    reduce_scatter x8, waiting for transfers between devices, __call__(): lax.psum_scatter(g, 'shard', scatter_dimension=0, tiled=True)  34.9 us
    unnamed x186, local copies, waits for them, and re-layouts  28.8 us
    sub x7, other arithmetic, adam(): weight - rate * (first_hat / (jnp.sqrt(second_hat) + 1e-08) + decay * wei...  28.6 us
    pallas_call x2, Pallas kernels, attend_fwd(): pl.pallas_call(attend_fwd_kernel, grid=(pairs, images), in_specs=[pl.Bloc...  26.7 us
  transfers between devices with their start and end apart: 19, of which 9 were waited for; matrix products, arithmetic and copies ran while one was open for 21% of the time, Pallas kernels for 10%

profile of v1, /device:TPU:0, one launch (start us, length us, event | category | flops | bytes accessed | tf_op | source)
XLA Modules:
  0.0 923.9 jit_solution(11249445425122984735)
XLA Ops:
  7.3 2.2 convert.24
  10.7 2.5 convert.26
  13.2 1.5 fusion.97
  14.8 2.5 convert.27
  22.5 3.6 all-reduce.6
  35.6 2.3 all-gather.2
  38.0 2.3 all-gather.6
  40.3 2.0 fusion.30
  43.9 2.3 convert_reduce_fusion.4
  46.2 2.0 maximum_select_fusion
  48.3 4.9 fusion.10.c_ref
  53.2 13.4 %shard_map.425 = bf16[1344,512]{1,0:T(8,128)(2,1)S(1)} custom-call(bf16[1344,1536]{1,0:T(8,128)(2,1)S(1)} %fusion.10.c_ref, f32[2,1792,128]{2,1,0:T(8,128)S(1)} %bitcast.203), custom_call_target="tpu_custom_call" | custom-call | flops 1409286144 | bytes 8028160 | tf_op jit(solution)/shard_map/pallas_call | solution.py:109
  67.8 1.5 copy-done.34
  69.9 10.2 %multiply_convert_fusion.3 = (bf16[1344,2048]{1,0:T(8,128)(2,1)}, f32[1344,2048]{1,0:T(8,128)}) fusion(f32[2048]{0:T(1024)S(1)} %bitcast.258, bf16[1,512,2048]{2,1,0:T(8,128)(2,1)} %all-gather.18.cloned.1.call-done, f32[1344,512]{1,0:T(8,128)} %copy-done.34, f32[512]{0:T(512)S(1)} %bitcast.277, f32[512]{0:T(512)S(1)} %bitcast.246, ...), kind=kOutput, calls=%fused_computation.18 | convolution fusion | flops 2838528000 | bytes 21387776 | tf_op jit(solution)/shard_map/dot_general | solution.py:21
  80.1 7.0 fusion.22
  87.1 1.7 convert_reduce_fusion.8
  88.9 2.1 multiply_reduce_fusion.9
  91.1 3.3 fusion.29
  94.4 4.7 fusion.11.c_ref
  99.1 13.3 %shard_map.426 = bf16[1344,512]{1,0:T(8,128)(2,1)S(1)} custom-call(bf16[1344,1536]{1,0:T(8,128)(2,1)S(1)} %fusion.11.c_ref, f32[2,1792,128]{2,1,0:T(8,128)S(1)} %bitcast.205), custom_call_target="tpu_custom_call" | custom-call | flops 1409286144 | bytes 8028160 | tf_op jit(solution)/shard_map/pallas_call | solution.py:109
  113.5 1.5 copy-done.31
  115.6 10.2 %multiply_convert_fusion.2 = (bf16[1344,2048]{1,0:T(8,128)(2,1)}, f32[1344,2048]{1,0:T(8,128)}) fusion(f32[2048]{0:T(1024)S(1)} %bitcast.260, bf16[1,512,2048]{2,1,0:T(8,128)(2,1)} %all-gather.24.cloned.1.call-done, f32[1344,512]{1,0:T(8,128)} %copy-done.31, f32[512]{0:T(512)S(1)} %bitcast.281, f32[512]{0:T(512)S(1)} %bitcast.254, ...), kind=kOutput, calls=%fused_computation.16 | convolution fusion | flops 2838528000 | bytes 21387776 | tf_op jit(solution)/shard_map/dot_general | solution.py:21
  125.8 9.4 %convert_reduce_fusion = (f32[2048]{0:T(1024)S(1)}, bf16[1344,2048]{1,0:T(8,128)(2,1)S(1)}) fusion(f32[1344,2048]{1,0:T(8,128)} %get-tuple-element.200, f32[2048]{0:T(1024)S(1)} %bitcast.261, bf16[1344,512]{1,0:T(8,128)(2,1)} %bitcast.211, bf16[1,2048,512]{2,1,0:T(8,128)(2,1)} %all-gather.26.cloned.1.call-done), kind=kOutput, calls=%fused_computation.12 | convolution fusion | flops 2859857920 | bytes 20004864 | tf_op jit(solution)/shard_map/dot_general | solution.py:21
  135.2 2.4 copy-done.87
  137.5 5.1 convolution_convert_fusion.6
  142.6 7.7 convolution_convert_fusion.7
  151.6 8.0 multiply_reduce_fusion
  162.3 1.6 copy-done.3
  163.9 30.7 %shard_map.427 = (bf16[1344,1536]{1,0:T(8,128)(2,1)S(1)}, f32[1792,128]{1,0:T(8,128)S(1)}) custom-call(bf16[1344,1536]{1,0:T(8,128)(2,1)S(1)} %copy-done.7, bf16[1344,512]{1,0:T(8,128)(2,1)S(1)} %convolution_convert_fusion.1.da_ref, f32[2,1792,128]{2,1,0:T(8,128)S(1)} %bitcast.206), custom_call_target="tpu_custom_call" | custom-call | flops 3523215360 | bytes 12156928 | tf_op jit(solution)/shard_map/pallas_call | solution.py:132
  194.7 2.0 copy-done.8
  196.6 1.8 convolution_convert_fusion.14
  198.4 6.8 convolution_convert_fusion.3
  206.1 7.1 fusion.83
  216.2 7.3 convolution_convert_fusion.5
  223.6 9.9 %convert_reduce_fusion.1 = (f32[2048]{0:T(1024)S(1)}, bf16[1344,2048]{1,0:T(8,128)(2,1)S(1)}) fusion(f32[1344,2048]{1,0:T(8,128)} %get-tuple-element.194, f32[2048]{0:T(1024)S(1)} %bitcast.259, bf16[1344,512]{1,0:T(8,128)(2,1)} %bitcast.214, bf16[1,2048,512]{2,1,0:T(8,128)(2,1)} %all-gather.20.cloned.1.call-done), kind=kOutput, calls=%fused_computation.13 | convolution fusion | flops 2859857920 | bytes 20004864 | tf_op jit(solution)/shard_map/dot_general | solution.py:21
  233.5 2.4 copy-done.88
  235.9 5.1 convolution_convert_fusion.4
  241.1 8.2 multiply_reduce_fusion.2
  250.7 1.5 copy-done.20
  252.3 2.0 convolution_convert_fusion.da_ref
  254.6 2.2 copy-done.5
  258.1 30.7 %shard_map.428 = (bf16[1344,1536]{1,0:T(8,128)(2,1)S(1)}, f32[1792,128]{1,0:T(8,128)S(1)}) custom-call(bf16[1344,1536]{1,0:T(8,128)(2,1)S(1)} %copy-done.5, bf16[1344,512]{1,0:T(8,128)(2,1)S(1)} %copy-done.15, f32[2,1792,128]{2,1,0:T(8,128)S(1)} %bitcast.204), custom_call_target="tpu_custom_call" | custom-call | flops 3523215360 | bytes 12156928 | tf_op jit(solution)/shard_map/pallas_call | solution.py:132
  288.8 2.0 copy-done.10
  290.8 1.8 convolution_convert_fusion.13
  292.6 6.9 convolution_convert_fusion.2
  299.6 8.0 fusion.82
  307.7 3.0 convert_reduce_fusion.3
  314.1 47.3 %all-reduce.25.cloned.1.call-done = (bf16[256,2048]{1,0:T(8,128)(2,1)}, bf16[1024,512]{1,0:T(8,128)(2,1)}) async-done(((bf16[256,2048]{1,0:T(8,128)(2,1)}, bf16[1024,512]{1,0:T(8,128)(2,1)}), (bf16[256,2048]{1,0:T(8,128)(2,1)}, bf16[1024,512]{1,0:T(8,128)(2,1)})) %all-reduce.25.cloned.1.call-update) | async-done | bytes 2097168 | tf_op jit(solution)/shard_map/psum | solution.py:283
  363.9 7.0 fusion.23
  371.0 1.5 convolution_convert_fusion.12
  373.2 13.6 %reduce-scatter.15.cloned.1.call-done = bf16[1024,512]{1,0:T(8,128)(2,1)} async-done(((bf16[2048,512]{1,0:T(8,128)(2,1)}), bf16[1024,512]{1,0:T(8,128)(2,1)}) %reduce-scatter.15.cloned.1.call-update) | async-done | bytes 1048592 | tf_op jit(solution)/shard_map/reduce_scatter | solution.py:279
  386.8 119.3 %all-reduce.23.cloned.1.call-done = (bf16[256,1536]{1,0:T(8,128)(2,1)}, bf16[256,512]{1,0:T(8,128)(2,1)}) async-done(((bf16[256,1536]{1,0:T(8,128)(2,1)}, bf16[256,512]{1,0:T(8,128)(2,1)}), (bf16[256,1536]{1,0:T(8,128)(2,1)}, bf16[256,512]{1,0:T(8,128)(2,1)})) %all-reduce.23.cloned.1.call-update) | async-done | bytes 1048592 | tf_op jit(solution)/shard_map/psum | solution.py:283
  506.2 3.2 add_convert_fusion
  509.5 1.9 fusion.64
  511.5 118.6 %all-reduce.17.cloned.1.call-done = f32[2,8848]{1,0:T(2,128)} async-done(((f32[2,8848]{1,0:T(2,128)}), f32[2,8848]{1,0:T(2,128)}) %all-reduce.17.cloned.1.call-update) | async-done | bytes 70800 | tf_op jit(solution)/shard_map/psum | solution.py:401
  635.1 7.6 reduce-scatter.11.cloned.1.call-done
  642.8 12.9 %reduce-scatter.9.cloned.1.call-done = bf16[256,1536]{1,0:T(8,128)(2,1)} async-done(((bf16[512,1536]{1,0:T(8,128)(2,1)}), bf16[256,1536]{1,0:T(8,128)(2,1)}) %reduce-scatter.9.cloned.1.call-update) | async-done | bytes 786448 | tf_op jit(solution)/shard_map/reduce_scatter | solution.py:279
  655.7 133.8 %all-reduce.21.cloned.1.call-done = (bf16[256,2048]{1,0:T(8,128)(2,1)}, bf16[1024,512]{1,0:T(8,128)(2,1)}) async-done(((bf16[256,2048]{1,0:T(8,128)(2,1)}, bf16[1024,512]{1,0:T(8,128)(2,1)}), (bf16[256,2048]{1,0:T(8,128)(2,1)}, bf16[1024,512]{1,0:T(8,128)(2,1)})) %all-reduce.21.cloned.1.call-update) | async-done | bytes 2097168 | tf_op jit(solution)/shard_map/psum | solution.py:283
  789.6 11.0 %multiply_subtract_fusion = (f32[2,1024,512]{2,1,0:T(8,128)}, f32[2,1024,512]{2,1,0:T(8,128)}, f32[2,1024,512]{2,1,0:T(8,128)}) fusion(f32[2,1024,512]{2,1,0:T(8,128)} %param.40, bf16[1,1024,512]{2,1,0:T(8,128)(2,1)S(1)} %bitcast.220, bf16[1,1024,512]{2,1,0:T(8,128)(2,1)} %bitcast.222, f32[2,1024,512]{2,1,0:T(8,128)} %param.42, f32[2,1024,512]{2,1,0:T(8,128)} %param.41), kind=kLoop, calls=%fused_computation.35 | loop fusion | flops 17825792 | bytes 27262976 | tf_op jit(solution)/shard_map/sub | solution.py:292
  800.7 1.8 copy-done.43
  803.0 6.2 multiply_subtract_fusion.1
  809.3 97.0 %all-reduce.19.cloned.1.call-done = (bf16[1,256,1536]{2,1,0:T(8,128)(2,1)}, bf16[1,256,512]{2,1,0:T(8,128)(2,1)}) async-done(((bf16[1,256,1536]{2,1,0:T(8,128)(2,1)}, bf16[1,256,512]{2,1,0:T(8,128)(2,1)}), (bf16[1,256,1536]{2,1,0:T(8,128)(2,1)}, bf16[1,256,512]{2,1,0:T(8,128)(2,1)})) %all-reduce.19.cloned.1.call-update) | async-done | bytes 1048592 | tf_op jit(solution)/shard_map/psum | solution.py:283
  906.3 3.4 multiply_subtract_fusion.3
  910.3 6.6 multiply_subtract_fusion.2
  (329 shorter events, 43.7 us)
Async XLA Ops:
  7.2 24.7 %copy-start = (bf16[6,196,512]{2,1,0:T(8,128)(2,1)S(1)}, bf16[6,196,512]{2,1,0:T(8,128)(2,1)}, u32[]{:S(2)}) copy-start(bf16[6,196,512]{2,1,0:T(8,128)(2,1)} %param.26) | copy-start | bytes 3612676
  7.2 41.1 %all-gather.16.cloned.1.call-start = ((), (), s32[]{:S(2)}) async-start(), calls=%async_computation.17 | async-start | bytes 2359296 | tf_op jit(solution)/shard_map/all_gather | solution.py:345
  10.7 59.2 %all-gather.18.cloned.1.call-start = ((), (), s32[]{:S(2)}) async-start(), calls=%async_computation.18 | async-start | bytes 3145728 | tf_op jit(solution)/shard_map/all_gather | solution.py:345
  14.7 65.4 %all-gather.20.cloned.1.call-start = ((), (), s32[]{:S(2)}) async-start(), calls=%async_computation.19 | async-start | bytes 3145728 | tf_op jit(solution)/shard_map/all_gather | solution.py:345
  18.7 7.8 copy-start.84
  18.7 11.6 %copy-start.80 = (s32[2,196]{1,0:T(2,128)S(1)}, s32[2,196]{1,0:T(2,128)}, u32[]{:S(2)}) copy-start(s32[2,196]{1,0:T(2,128)} %param.28) | copy-start | bytes 4708
  18.7 75.6 %all-gather.22.cloned.1.call-start = ((), (), s32[]{:S(2)}) async-start(), calls=%async_computation.20 | async-start | bytes 2359296 | tf_op jit(solution)/shard_map/all_gather | solution.py:345
  19.3 96.3 %all-gather.24.cloned.1.call-start = ((), (), s32[]{:S(2)}) async-start(), calls=%async_computation.21 | async-start | bytes 3145728 | tf_op jit(solution)/shard_map/all_gather | solution.py:345
  19.9 105.9 %all-gather.26.cloned.1.call-start = ((), (), s32[]{:S(2)}) async-start(), calls=%async_computation.22 | async-start | bytes 3145728 | tf_op jit(solution)/shard_map/all_gather | solution.py:345
  20.5 203.0 %reduce-scatter.21.cloned.1.call-start = ((), (), s32[]{:S(2)}) async-start(), calls=%async_computation.14 | async-start | bytes 3145728 | tf_op jit(solution)/shard_map/reduce_scatter | solution.py:279
  31.1 12.3 %copy-start.56 = (bf16[224,196]{0,1:T(8,128)(2,1)}, bf16[224,196]{0,1:T(8,128)(2,1)S(1)}, u32[]{:S(2)}) copy-start(bf16[224,196]{0,1:T(8,128)(2,1)S(1)} %fusion.69) | copy-start | bytes 263428
  32.6 7.7 copy-start.24
  32.7 7.6 copy-start.58
  53.2 13.5 %copy-start.4 = (bf16[1344,1536]{1,0:T(8,128)(2,1)}, bf16[1344,1536]{1,0:T(8,128)(2,1)S(1)}, u32[]{:S(2)}) copy-start(bf16[1344,1536]{1,0:T(8,128)(2,1)S(1)} %fusion.10.c_ref) | copy-start | bytes 12386308
  53.2 13.5 %copy-start.25 = (bf16[6,224,512]{2,1,0:T(8,128)(2,1)S(1)}, bf16[6,224,512]{2,1,0:T(8,128)(2,1)}, u32[]{:S(2)}) copy-start(bf16[6,224,512]{2,1,0:T(8,128)(2,1)} %copy-done.24) | copy-start | bytes 4128772
  53.2 13.5 %copy-start.45 = (bf16[1,512,512]{2,1,0:T(8,128)(2,1)S(1)}, bf16[1,512,512]{2,1,0:T(8,128)(2,1)}, u32[]{:S(2)}) copy-start(bf16[1,512,512]{2,1,0:T(8,128)(2,1)} %all-gather.2) | copy-start | bytes 1572868
  99.1 13.3 %copy-start.6 = (bf16[1344,1536]{1,0:T(8,128)(2,1)}, bf16[1344,1536]{1,0:T(8,128)(2,1)S(1)}, u32[]{:S(2)}) copy-start(bf16[1344,1536]{1,0:T(8,128)(2,1)S(1)} %fusion.11.c_ref) | copy-start | bytes 12386308
  99.1 13.3 %copy-start.27 = (bf16[6,224,512]{2,1,0:T(8,128)(2,1)S(1)}, bf16[6,224,512]{2,1,0:T(8,128)(2,1)}, u32[]{:S(2)}) copy-start(bf16[6,224,512]{2,1,0:T(8,128)(2,1)} %get-tuple-element.196) | copy-start | bytes 4128772
  99.1 13.3 %copy-start.47 = (bf16[1,512,512]{2,1,0:T(8,128)(2,1)S(1)}, bf16[1,512,512]{2,1,0:T(8,128)(2,1)}, u32[]{:S(2)}) copy-start(bf16[1,512,512]{2,1,0:T(8,128)(2,1)} %all-gather.6) | copy-start | bytes 1572868
  125.8 11.7 %copy-start.32 = (f32[1344,512]{1,0:T(8,128)S(1)}, f32[1344,512]{1,0:T(8,128)}, u32[]{:S(2)}) copy-start(f32[1344,512]{1,0:T(8,128)} %copy-done.31) | copy-start | bytes 8257540
  150.4 73.1 %reduce-scatter.23.cloned.1.call-start = ((), (), s32[]{:S(2)}) async-start(), calls=%async_computation.15 | async-start | bytes 3145728 | tf_op jit(solution)/shard_map/reduce_scatter | solution.py:279
  151.2 162.9 %reduce-scatter.19.cloned.1.call-start = ((), (), s32[]{:S(2)}) async-start(), calls=%async_computation.13 | async-start | bytes 786432 | tf_op jit(solution)/shard_map/reduce_scatter | solution.py:279
  151.6 8.1 copy-start.33
  151.6 8.1 copy-start.37
  161.1 33.5 %copy-start.22 = (f32[1344,512]{1,0:T(8,128)}, f32[1344,512]{1,0:T(8,128)S(1)}, u32[]{:S(2)}) copy-start(f32[1344,512]{1,0:T(8,128)S(1)} %get-tuple-element.134) | copy-start | bytes 8257540
  163.9 32.7 %copy-start.14 = (bf16[1344,512]{1,0:T(8,128)(2,1)S(1)}, bf16[1344,512]{1,0:T(8,128)(2,1)}, u32[]{:S(2)}) copy-start(bf16[1344,512]{1,0:T(8,128)(2,1)} %copy-done.13) | copy-start | bytes 4128772
  205.3 108.8 %reduce-scatter.17.cloned.1.call-start = ((), (), s32[]{:S(2)}) async-start(), calls=%async_computation.12 | async-start | bytes 2359296 | tf_op jit(solution)/shard_map/reduce_scatter | solution.py:279
  205.9 155.5 %all-reduce.25.cloned.1.call-start = ((), (), s32[]{:S(2)}) async-start(), calls=%async_computation.26 | async-start | bytes 4194304 | tf_op jit(solution)/shard_map/psum | solution.py:283
  206.1 7.2 copy-start.23
  206.1 7.2 copy-start.28
  223.5 149.7 %reduce-scatter.13.cloned.1.call-start = ((), (), s32[]{:S(2)}) async-start(), calls=%async_computation.10 | async-start | bytes 3145728 | tf_op jit(solution)/shard_map/reduce_scatter | solution.py:279
  223.6 12.4 %copy-start.35 = (f32[1344,512]{1,0:T(8,128)S(1)}, f32[1344,512]{1,0:T(8,128)}, u32[]{:S(2)}) copy-start(f32[1344,512]{1,0:T(8,128)} %copy-done.34) | copy-start | bytes 8257540
  241.0 145.8 %reduce-scatter.15.cloned.1.call-start = ((), (), s32[]{:S(2)}) async-start(), calls=%async_computation.11 | async-start | bytes 3145728 | tf_op jit(solution)/shard_map/reduce_scatter | solution.py:279
  241.1 8.2 copy-start.36
  241.1 8.2 copy-start.39
  254.3 251.8 %all-reduce.23.cloned.1.call-start = ((), (), s32[]{:S(2)}) async-start(), calls=%async_computation.25 | async-start | bytes 2097152 | tf_op jit(solution)/shard_map/psum | solution.py:283
  258.1 32.7 %copy-start.12 = (bf16[1344,512]{1,0:T(8,128)(2,1)S(1)}, bf16[1344,512]{1,0:T(8,128)(2,1)}, u32[]{:S(2)}) copy-start(bf16[1344,512]{1,0:T(8,128)(2,1)} %copy-done.11) | copy-start | bytes 4128772
  258.1 32.7 %copy-start.21 = (f32[1344,512]{1,0:T(8,128)S(1)}, f32[1344,512]{1,0:T(8,128)}, u32[]{:S(2)}) copy-start(f32[1344,512]{1,0:T(8,128)} %copy-done.20) | copy-start | bytes 8257540
  299.6 8.0 copy-start.74
  312.6 51.3 %copy-start.79 = (f32[1,1,512]{2,0,1:T(1,128)S(1)}, f32[1,1,512]{2,0,1:T(1,128)}, u32[]{:S(2)}) copy-start(f32[1,1,512]{2,0,1:T(1,128)} %get-tuple-element.163) | copy-start | bytes 6148
  361.4 268.6 %all-reduce.17.cloned.1.call-start = ((), (), s32[]{:S(2)}) async-start(), calls=%async_computation.16 | async-start | bytes 143360 | tf_op jit(solution)/shard_map/psum | solution.py:401
  362.4 280.3 %reduce-scatter.11.cloned.1.call-start = ((), (), s32[]{:S(2)}) async-start(), calls=%async_computation.9 | async-start | bytes 786432 | tf_op jit(solution)/shard_map/reduce_scatter | solution.py:279
  363.0 292.6 %reduce-scatter.9.cloned.1.call-start = ((), (), s32[]{:S(2)}) async-start(), calls=%async_computation.8 | async-start | bytes 2359296 | tf_op jit(solution)/shard_map/reduce_scatter | solution.py:279
  363.6 425.9 %all-reduce.21.cloned.1.call-start = ((), (), s32[]{:S(2)}) async-start(), calls=%async_computation.24 | async-start | bytes 4194304 | tf_op jit(solution)/shard_map/psum | solution.py:283
  363.9 7.0 copy-start.57
  506.1 400.1 %all-reduce.19.cloned.1.call-start = ((), (), s32[]{:S(2)}) async-start(), calls=%async_computation.23 | async-start | bytes 2097152 | tf_op jit(solution)/shard_map/psum | solution.py:283
  509.4 121.5 %copy-start.65 = (f32[2,6,256]{2,0,1:T(2,128)S(1)}, f32[2,6,256]{2,0,1:T(2,128)}, u32[]{:S(2)}) copy-start(f32[2,6,256]{2,0,1:T(2,128)} %param.46) | copy-start | bytes 36868
  509.4 121.5 %copy-start.70 = (f32[2,6,256]{2,0,1:T(2,128)S(1)}, f32[2,6,256]{2,0,1:T(2,128)}, u32[]{:S(2)}) copy-start(f32[2,6,256]{2,0,1:T(2,128)} %param.48) | copy-start | bytes 36868
  509.4 121.5 %copy-start.71 = (f32[2,6,256]{2,0,1:T(2,128)S(1)}, f32[2,6,256]{2,0,1:T(2,128)}, u32[]{:S(2)}) copy-start(f32[2,6,256]{2,0,1:T(2,128)} %param.47) | copy-start | bytes 36868
  509.4 124.3 %copy-start.63 = (f32[2,8,169]{2,1,0:T(8,128)S(1)}, f32[2,8,169]{2,1,0:T(8,128)}, u32[]{:S(2)}) copy-start(f32[2,8,169]{2,1,0:T(8,128)} %param.43) | copy-start | bytes 32452
  509.5 124.3 %copy-start.68 = (f32[2,8,169]{2,1,0:T(8,128)S(1)}, f32[2,8,169]{2,1,0:T(8,128)}, u32[]{:S(2)}) copy-start(f32[2,8,169]{2,1,0:T(8,128)} %param.45) | copy-start | bytes 32452
  509.5 124.3 %copy-start.69 = (f32[2,8,169]{2,1,0:T(8,128)S(1)}, f32[2,8,169]{2,1,0:T(8,128)}, u32[]{:S(2)}) copy-start(f32[2,8,169]{2,1,0:T(8,128)} %param.44) | copy-start | bytes 32452
  509.5 125.0 %copy-start.67 = (f32[2,1536]{1,0:T(2,128)S(1)}, f32[2,1536]{1,0:T(2,128)}, u32[]{:S(2)}) copy-start(f32[2,1536]{1,0:T(2,128)} %param.49) | copy-start | bytes 36868
  509.5 125.0 %copy-start.72 = (f32[2,1536]{1,0:T(2,128)S(1)}, f32[2,1536]{1,0:T(2,128)}, u32[]{:S(2)}) copy-start(f32[2,1536]{1,0:T(2,128)} %param.51) | copy-start | bytes 36868
  509.5 125.0 %copy-start.73 = (f32[2,1536]{1,0:T(2,128)S(1)}, f32[2,1536]{1,0:T(2,128)}, u32[]{:S(2)}) copy-start(f32[2,1536]{1,0:T(2,128)} %param.50) | copy-start | bytes 36868
  509.5 280.0 %copy-start.52 = (bf16[1024,512]{1,0:T(8,128)(2,1)S(1)}, bf16[1024,512]{1,0:T(8,128)(2,1)}, u32[]{:S(2)}) copy-start(bf16[1024,512]{1,0:T(8,128)(2,1)} %get-tuple-element.121) | copy-start | bytes 3145732
  789.6 11.0 %copy-start.29 = (f32[2,256,2048]{2,1,0:T(8,128)S(1)}, f32[2,256,2048]{2,1,0:T(8,128)}, u32[]{:S(2)}) copy-start(f32[2,256,2048]{2,1,0:T(8,128)} %param.37) | copy-start | bytes 12582916
  789.6 11.1 %copy-start.42 = (f32[2,256,2048]{2,1,0:T(8,128)S(1)}, f32[2,256,2048]{2,1,0:T(8,128)}, u32[]{:S(2)}) copy-start(f32[2,256,2048]{2,1,0:T(8,128)} %param.39) | copy-start | bytes 12582916
  789.6 12.9 %copy-start.43 = (f32[2,256,2048]{2,1,0:T(8,128)S(1)}, f32[2,256,2048]{2,1,0:T(8,128)}, u32[]{:S(2)}) copy-start(f32[2,256,2048]{2,1,0:T(8,128)} %param.38) | copy-start | bytes 12582916
  789.6 13.1 %copy-start.51 = (bf16[256,2048]{1,0:T(8,128)(2,1)S(1)}, bf16[256,2048]{1,0:T(8,128)(2,1)}, u32[]{:S(2)}) copy-start(bf16[256,2048]{1,0:T(8,128)(2,1)} %get-tuple-element.120) | copy-start | bytes 3145732
  789.6 13.4 %copy-start.53 = (bf16[256,2048]{1,0:T(8,128)(2,1)S(1)}, bf16[256,2048]{1,0:T(8,128)(2,1)}, u32[]{:S(2)}) copy-start(bf16[256,2048]{1,0:T(8,128)(2,1)} %get-tuple-element.116) | copy-start | bytes 3145732
  803.0 103.2 %copy-start.41 = (f32[2,256,512]{2,1,0:T(8,128)S(1)}, f32[2,256,512]{2,1,0:T(8,128)}, u32[]{:S(2)}) copy-start(f32[2,256,512]{2,1,0:T(8,128)} %param.34) | copy-start | bytes 3145732
  803.0 103.2 %copy-start.49 = (f32[2,256,512]{2,1,0:T(8,128)S(1)}, f32[2,256,512]{2,1,0:T(8,128)}, u32[]{:S(2)}) copy-start(f32[2,256,512]{2,1,0:T(8,128)} %param.36) | copy-start | bytes 3145732
  803.0 103.2 %copy-start.50 = (f32[2,256,512]{2,1,0:T(8,128)S(1)}, f32[2,256,512]{2,1,0:T(8,128)}, u32[]{:S(2)}) copy-start(f32[2,256,512]{2,1,0:T(8,128)} %param.35) | copy-start | bytes 3145732
  (44 other events, 119.6 us)
Sparse Core Ops, SparseCore 0:
  10.8 12.4 all-gather.15
  25.5 11.7 all-gather.17
  39.4 11.7 all-gather.19
  53.1 11.0 all-gather.21
  66.2 11.7 all-gather.23
  80.0 11.7 all-gather.25
  150.5 11.4 reduce-scatter.20
  165.0 10.8 reduce-scatter.22
  205.4 9.7 reduce-scatter.18
  218.0 10.2 reduce-scatter.16
  233.8 127.5 all-reduce.24
  364.2 8.9 reduce-scatter.12
  376.0 10.7 reduce-scatter.14
  392.9 113.1 all-reduce.22
  513.0 117.0 all-reduce.16
  632.8 9.8 reduce-scatter.10
  645.4 10.1 reduce-scatter.8
  662.0 127.5 all-reduce.20
  794.9 111.3 all-reduce.18
